TPU v7x, 512 devices: a whole 4x8x8 slice. The times are simulated.
512 devices in a mesh: section: 8 (over x, core), dp: 64 (over y, z).
Axes of the slice: x: 4, y: 8, z: 8, core: 2. Of those that a mesh axis runs over, the one named last changes fastest.
Arguments:
- gradients: bfloat16 [8, 64, 192, 3072], P('section', 'dp'), may hold values from -800 to 800
- error_buffers: bfloat16 [8, 64, 192, 3072], P('section', 'dp'), may hold values from -6 to 6
- initial_q: float32 [8, 192, 32], P('section'), may hold values from -6 to 6
- master: float32 [8, 192, 3072], P('section', None, 'dp'), may hold values from -0.75 to 0.75
- first_moment: float32 [8, 192, 3072], P('section', None, 'dp'), may hold values from -0.046875 to 0.046875
- second_moment: float32 [8, 192, 3072], P('section', None, 'dp'), may hold values from 1e-07 to 1e-05
Outputs:
- new_errors: bfloat16 [8, 64, 192, 3072], P('section', 'dp')
- q_factor: float32 [8, 192, 32], P('section')
- new_master: float32 [8, 192, 3072], P('section', None, 'dp')
- new_first: float32 [8, 192, 3072], P('section', None, 'dp')
- new_second: float32 [8, 192, 3072], P('section', None, 'dp')
- gathered_weights: bfloat16 [8, 192, 3072], P('section')
All inputs are finite; a program needn't handle non-finite values.
Results may differ from a plain program's by a relative error of at most 0.00045.
Values may be sent and summed in bfloat16 or wider, within the bound.
A program may use at most 64 MiB of HBM per device.

v0:
```python
import jax
import jax.numpy as jnp
from jax import lax
from jax.sharding import PartitionSpec as P

STEP = 10


beta_one = 0.9
beta_two = 0.999
adam_epsilon = 1e-08
learn_rate = 0.02
clip_limit = 16.0


def basis_from(gram_matrix, block):
    cholesky_factor = jnp.linalg.cholesky(gram_matrix)
    solved = jax.scipy.linalg.solve_triangular(cholesky_factor, block.T, lower=True)
    return solved.T


def per_device(gradients, error_buffers, initial_q, master, first_moment, second_moment):
    combined = gradients[0, 0].astype(jnp.float32) + error_buffers[0, 0].astype(jnp.float32)
    start_q = initial_q[0]
    replicas = lax.axis_size("dp")
    owned_cols = master.shape[2]
    first_col = lax.axis_index("dp") * owned_cols
    local_power = jnp.dot(combined.T, start_q, precision=lax.Precision.HIGHEST)
    projected = lax.psum(local_power, "dp")
    gram_matrix = jnp.dot(projected.T, projected, precision=lax.Precision.HIGHEST)
    ortho_basis = basis_from(gram_matrix, projected)
    owned_basis = lax.dynamic_slice_in_dim(ortho_basis, first_col, owned_cols, 0)
    local_right = jnp.dot(combined, ortho_basis, precision=lax.Precision.HIGHEST)
    right_factor = lax.psum(local_right, "dp") / replicas
    approx = jnp.dot(right_factor, ortho_basis.T, precision=lax.Precision.HIGHEST)
    new_errors = (combined - approx).astype(jnp.bfloat16)
    owned_grad = jnp.dot(right_factor, owned_basis.T, precision=lax.Precision.HIGHEST)
    squares = lax.psum(jnp.sum(owned_grad * owned_grad), ("section", "dp"))
    clip_factor = jnp.minimum(1.0, clip_limit / jnp.sqrt(squares))
    scaled = clip_factor * owned_grad
    new_first = beta_one * first_moment[0] + (1.0 - beta_one) * scaled
    new_second = beta_two * second_moment[0] + (1.0 - beta_two) * scaled * scaled
    adam_step = (
        new_first
        / (1.0 - beta_one**STEP)
        / (jnp.sqrt(new_second / (1.0 - beta_two**STEP)) + adam_epsilon)
    )
    new_master = master[0] - learn_rate * adam_step
    gathered_weights = lax.all_gather(new_master.astype(jnp.bfloat16), "dp", axis=1, tiled=True)
    return (
        new_errors[None, None],
        right_factor[None],
        new_master[None],
        new_first[None],
        new_second[None],
        gathered_weights[None],
    )


def solution(mesh):
    placed = (
        P("section", "dp", None, None),
        P("section", "dp", None, None),
        P("section", None, None),
        P("section", None, "dp"),
        P("section", None, "dp"),
        P("section", None, "dp"),
    )
    return jax.shard_map(
        per_device,
        mesh=mesh,
        in_specs=placed,
        out_specs=(
            P("section", "dp", None, None),
            P("section", None, None),
            P("section", None, "dp"),
            P("section", None, "dp"),
            P("section", None, "dp"),
            P("section", None, None),
        ),
        check_vma=False,
    )
```

profile of v0, /device:TPU:1, one launch (start us, length us, event | category | flops | bytes accessed | tf_op | source)
XLA Modules:
  0.0 641.4 jit_solution(4714943307280041799)
XLA Ops:
  7.2 0.0 copy-start
  7.2 0.0 all-reduce.2.cloned.1.call-start
  7.2 0.7 copy-done
  7.9 4.3 fusion.4
  12.2 0.0 all-reduce.2.cloned.1.call-update
  12.2 0.0 all-gather.2.cloned.1.call-start
  12.3 156.2 %all-reduce.2.cloned.1.call-done = f32[3072,32]{0,1:T(8,128)} async-done(((f32[3072,32]{0,1:T(8,128)}), f32[3072,32]{0,1:T(8,128)}) %all-reduce.2.cloned.1.call-update) | async-done | bytes 393232 | tf_op jit(solution)/shard_map/psum | solution.py:29
  168.4 1.6 fusion.24
  170.0 0.1 copy.12
  170.1 2.9 cholesky.16
  173.0 0.6 compare_reduce_fusion
  173.7 0.7 fusion.11
  174.4 2.4 custom-call.7
  176.8 1.5 fusion.12
  178.4 2.2 fusion.2
  180.6 222.2 %psum.22 = f32[192,32]{0,1:T(8,128)S(1)} all-reduce(f32[192,32]{0,1:T(8,128)S(1)} %fusion.2), channel_id=1, replica_groups=mesh['section'=8,'dp'=64] {'dp'}, use_global_device_ids=true, to_apply=%region_3.4 | all-reduce | flops 6144 | bytes 49152 | tf_op jit(solution)/shard_map/psum | solution.py:34
  402.8 0.9 multiply_reduce_fusion
  403.8 152.6 %psum.23 = f32[]{:T(128)} all-reduce(f32[]{:T(128)} %get-tuple-element.16), channel_id=1, replica_groups=mesh['section'=8,'dp'=64] {'section','dp'}, use_global_device_ids=true, to_apply=%region_5.6 | all-reduce | flops 1 | bytes 8 | tf_op jit(solution)/shard_map/psum | solution.py:38
  557.1 0.7 fusion.23
  557.8 0.0 all-gather.2.cloned.1.call-update
  557.8 0.6 multiply_bitcast_fusion
  558.4 3.2 fusion.1
  561.6 70.5 %all-gather.2.cloned.1.call-done = bf16[192,3072]{0,1:T(8,128)(2,1)} async-done(((bf16[192,48]{0,1:T(8,128)(2,1)}), bf16[192,3072]{0,1:T(8,128)(2,1)}) %all-gather.2.cloned.1.call-update) | async-done | bytes 1179664 | tf_op jit(solution)/shard_map/all_gather | solution.py:49
  632.1 2.5 copy.13
  (12 shorter events, 0.1 us)
Async XLA Ops:
  7.2 0.8 copy-start
  7.2 161.3 %all-reduce.2.cloned.1.call-start = ((), (), s32[]{:S(2)}) async-start(), calls=%async_computation | async-start | bytes 786432 | tf_op jit(solution)/shard_map/psum | solution.py:29
  7.9 170.4 %copy-start.2 = (bf16[1,1,192,3072]{3,2,1,0:T(8,128)(2,1)S(1)}, bf16[1,1,192,3072]{3,2,1,0:T(8,128)(2,1)}, u32[]{:S(2)}) copy-start(bf16[1,1,192,3072]{3,2,1,0:T(8,128)(2,1)} %param.6) | copy-start | bytes 3538948
  12.2 166.1 %copy-start.1 = (bf16[1,1,192,3072]{3,2,1,0:T(8,128)(2,1)S(1)}, bf16[1,1,192,3072]{3,2,1,0:T(8,128)(2,1)}, u32[]{:S(2)}) copy-start(bf16[1,1,192,3072]{3,2,1,0:T(8,128)(2,1)} %param.7) | copy-start | bytes 3538948
  12.2 619.9 %all-gather.2.cloned.1.call-start = ((), (), s32[]{:S(2)}) async-start(), calls=%async_computation.1 | async-start | bytes 1597440 | tf_op jit(solution)/shard_map/all_gather | solution.py:49
  178.4 378.7 %copy-start.3 = (f32[1,192,48]{1,2,0:T(8,128)S(1)}, f32[1,192,48]{1,2,0:T(8,128)}, u32[]{:S(2)}) copy-start(f32[1,192,48]{1,2,0:T(8,128)} %param.11) | copy-start | bytes 110596
  178.4 378.7 %copy-start.4 = (f32[1,192,48]{1,2,0:T(8,128)S(1)}, f32[1,192,48]{1,2,0:T(8,128)}, u32[]{:S(2)}) copy-start(f32[1,192,48]{1,2,0:T(8,128)} %param.10) | copy-start | bytes 110596
  178.4 378.7 %copy-start.5 = (f32[1,192,48]{1,2,0:T(8,128)S(1)}, f32[1,192,48]{1,2,0:T(8,128)}, u32[]{:S(2)}) copy-start(f32[1,192,48]{1,2,0:T(8,128)} %param.9) | copy-start | bytes 110596
Sparse Core Ops, SparseCore 0:
  12.4 156.0 all-reduce.1
  557.9 74.1 all-gather.1
where the time goes:
time: 645 us; the launch traced here: 641 us
  blocking collectives  375 us (58%)
  waiting for transfers between devices  227 us (35%)
  between operations  14.8 us (2%)
  matrix products  13.7 us (2%)
  other arithmetic  8.01 us (1%)
    psum x1, blocking collectives, per_device(): right_factor = lax.psum(local_right, 'dp') / replicas  222 us
    psum x1, waiting for transfers between devices, per_device(): projected = lax.psum(local_power, 'dp')  156 us
    psum x1, blocking collectives, per_device(): squares = lax.psum(jnp.sum(owned_grad * owned_grad), ('section', 'dp'))  153 us
    all_gather x1, waiting for transfers between devices, per_device(): lax.all_gather(new_master.astype(jnp.bfloat16), 'dp', axis=1, tiled=True)  70.5 us
  transfers between devices with their start and end apart: 2, of which 2 were waited for; matrix products, arithmetic and copies ran while one was open for 1% of the time, Pallas kernels for 0%

commit v1 on v0

v1 whole, which is shorter than its diff:
```python
import functools

import jax
import jax.numpy as jnp
from jax import lax
from jax.experimental import pallas as pl
from jax.experimental.pallas import tpu as pltpu
from jax.sharding import PartitionSpec as P

STEP = 10


beta_one = 0.9
beta_two = 0.999
adam_epsilon = 1e-08
learn_rate = 0.02
clip_limit = 16.0

RING = 8
ORDER = (4, 3, 5, 2, 6, 1, 7)
MESH = pl.DeviceIdType.MESH
HIGH = lax.Precision.HIGHEST
F32 = jnp.float32
BF16 = jnp.bfloat16


def dot_nn(a, b):
    return lax.dot_general(a, b, (((1,), (0,)), ((), ())), precision=HIGH, preferred_element_type=F32)


def dot_tn(a, b):
    return lax.dot_general(a, b, (((0,), (0,)), ((), ())), precision=HIGH, preferred_element_type=F32)


def dot_nt(a, b):
    return lax.dot_general(a, b, (((1,), (1,)), ((), ())), precision=HIGH, preferred_element_type=F32)


def three_parts(value):
    high = value.astype(BF16)
    rest = value - high.astype(F32)
    middle = rest.astype(BF16)
    low = (rest - middle.astype(F32)).astype(BF16)
    return high, middle, low


def lower_inverse(gram):
    rank = gram.shape[0]
    rows = lax.broadcasted_iota(jnp.int32, (rank, 128), 0)
    lanes = lax.broadcasted_iota(jnp.int32, (rank, 128), 1)
    identity = jnp.where(lanes == rows + rank, 1.0, 0.0).astype(F32)
    wide = jnp.concatenate([gram, jnp.zeros((rank, 128 - rank), F32)], axis=1) + identity
    pivots = jnp.ones((rank, 128), F32)
    for k in range(rank):
        column = jnp.broadcast_to(wide[:, k : k + 1], (rank, 128))
        pivot = jnp.broadcast_to(column[k : k + 1, :], (rank, 128))
        row = jnp.broadcast_to(wide[k : k + 1, :], (rank, 128))
        pivots = jnp.where(rows == k, pivot, pivots)
        factor = jnp.where(rows > k, column / pivot, 0.0)
        wide = wide - factor * row
    scaled = wide * lax.rsqrt(pivots)
    return scaled[:, rank : 2 * rank]


def step_kernel(
    g_ref, e_ref, q_ref, master_ref, first_ref, second_ref,
    err_ref, right_ref, new_master_ref, new_first_ref, new_second_ref, out_ref,
    local, red_a, red_b, sum_a, sum_b, full, fold, fold_a, fold_b, next_a, next_b, norm, norms,
    group, send_a, send_b, gat_a, gat_b, nat_a, tail_b, ss, rs,
):
    section = lax.axis_index("section")
    dp = lax.axis_index("dp")
    y = lax.div(dp, RING)
    z = lax.rem(dp, RING)
    replicas = RING * RING
    rank = q_ref.shape[0]
    half = rank // 2
    width = g_ref.shape[1] // RING
    owned = master_ref.shape[0]

    def up(i, d):
        return lax.rem(i + d, RING)

    def down(i, d):
        return lax.rem(i + RING - d, RING)

    def peer(axis, d):
        if axis == "z":
            return (section, y * RING + up(z, d))
        if axis == "y":
            return (section, up(y, d) * RING + z)
        return (up(section, d), dp)

    def copy(phase, lane, axis, d, src, dst):
        return pltpu.make_async_remote_copy(
            src_ref=src, dst_ref=dst, send_sem=ss.at[phase, lane, d], recv_sem=rs.at[phase, lane, d],
            device_id=peer(axis, d), device_id_type=MESH,
        )

    barrier = pltpu.get_barrier_semaphore()
    for axis in ("z", "y", "s"):
        for d in range(1, RING):
            pl.semaphore_signal(barrier, 1, device_id=peer(axis, d), device_id_type=MESH)

    parts = jnp.concatenate(three_parts(q_ref[...]), axis=0)
    for j in range(RING):
        cols = pl.ds(j * width, width)
        term = jnp.dot(parts, g_ref[:, cols], preferred_element_type=F32)
        term += jnp.dot(parts, e_ref[:, cols], preferred_element_type=F32)
        local[j] = term[:rank] + term[rank : 2 * rank] + term[2 * rank :]

    pl.semaphore_wait(barrier, 3 * (RING - 1))

    started = []

    def send(*args):
        c = copy(*args)
        c.start()
        started.append(c)

    for d in ORDER:
        send(0, 0, "z", d, local.at[up(z, d), pl.ds(0, half)], red_a.at[d - 1])
        send(0, 1, "y", d, local.at[up(y, d), pl.ds(half, half)], red_b.at[d - 1])
    total_a = local[z, 0:half]
    total_b = local[y, half:rank]
    for d in ORDER[::-1]:
        copy(0, 0, "z", d, red_a.at[d - 1], red_a.at[d - 1]).wait_recv()
        total_a += red_a[d - 1]
        copy(0, 1, "y", d, red_b.at[d - 1], red_b.at[d - 1]).wait_recv()
        total_b += red_b[d - 1]
    sum_a[y] = total_a
    sum_b[z] = total_b
    for d in ORDER:
        send(1, 0, "y", d, sum_a.at[y], sum_a.at[y])
        send(1, 1, "z", d, sum_b.at[z], sum_b.at[z])
    for d in ORDER[::-1]:
        copy(1, 0, "y", d, sum_a.at[down(y, d)], sum_a.at[down(y, d)]).wait_recv()
        copy(1, 1, "z", d, sum_b.at[down(z, d)], sum_b.at[down(z, d)]).wait_recv()
    total_a = sum_a[0]
    total_b = sum_b[0]
    for i in range(1, RING):
        total_a += sum_a[i]
        total_b += sum_b[i]
    full[z, 0:half] = total_a
    full[y, half:rank] = total_b
    for d in ORDER:
        send(2, 0, "z", d, full.at[z, pl.ds(0, half)], full.at[z, pl.ds(0, half)])
        send(2, 1, "y", d, full.at[y, pl.ds(half, half)], full.at[y, pl.ds(half, half)])
    for d in ORDER[::-1]:
        src_z, src_y = down(z, d), down(y, d)
        copy(2, 0, "z", d, full.at[src_z, pl.ds(0, half)], full.at[src_z, pl.ds(0, half)]).wait_recv()
        copy(2, 1, "y", d, full.at[src_y, pl.ds(half, half)], full.at[src_y, pl.ds(half, half)]).wait_recv()

    right = jnp.zeros((3 * rank, g_ref.shape[0]), F32)
    for j in range(RING):
        cols = pl.ds(j * width, width)
        parts = jnp.concatenate(three_parts(full[j]), axis=0)
        for source in (g_ref, e_ref):
            right += lax.dot_general(
                parts, source[:, cols], (((1,), (1,)), ((), ())), preferred_element_type=F32
            )
    right = right[:rank] + right[rank : 2 * rank] + right[2 * rank :]
    rest = jnp.concatenate([right[:half, 128:192], right[half:, 128:192]], axis=1)
    fold[0:16] = right[:half, :128]
    fold[16:24] = rest[:8]
    fold[24:40] = right[half:, :128]
    fold[40:48] = rest[8:]
    fold_a[z] = fold[0:24]
    fold_b[y] = fold[24:48]
    for d in ORDER:
        send(3, 0, "z", d, fold_a.at[z], fold_a.at[z])
        send(3, 1, "y", d, fold_b.at[y], fold_b.at[y])

    gram = jnp.zeros((rank, rank), F32)
    for j in range(RING):
        gram += dot_nt(full[j], full[j])
    inverse = lower_inverse(gram)

    for d in ORDER[::-1]:
        copy(3, 0, "z", d, fold_a.at[down(z, d)], fold_a.at[down(z, d)]).wait_recv()
        copy(3, 1, "y", d, fold_b.at[down(y, d)], fold_b.at[down(y, d)]).wait_recv()
    total_a = fold_a[0]
    total_b = fold_b[0]
    for i in range(1, RING):
        total_a += fold_a[i]
        total_b += fold_b[i]
    next_a[y] = total_a
    next_b[z] = total_b
    for d in ORDER:
        send(4, 0, "y", d, next_a.at[y], next_a.at[y])
        send(4, 1, "z", d, next_b.at[z], next_b.at[z])
    for d in ORDER[::-1]:
        copy(4, 0, "y", d, next_a.at[down(y, d)], next_a.at[down(y, d)]).wait_recv()
        copy(4, 1, "z", d, next_b.at[down(z, d)], next_b.at[down(z, d)]).wait_recv()
    total_a = next_a[0]
    total_b = next_b[0]
    for i in range(1, RING):
        total_a += next_a[i]
        total_b += next_b[i]
    rest = jnp.concatenate([total_a[16:24], total_b[16:24]], axis=0)
    top = jnp.concatenate([total_a[0:16], total_b[0:16]], axis=0)
    rest = jnp.concatenate([rest[:, :64], rest[:, 64:]], axis=0)
    right = jnp.concatenate([top, rest], axis=1)
    right = dot_nn(inverse, right) * (1.0 / replicas)
    right_ref[...] = right
    squares = jnp.sum(right * right, keepdims=True)
    norms[section] = jnp.broadcast_to(squares, (8, 128))
    for d in ORDER:
        send(5, 0, "s", d, norms.at[section], norms.at[section])

    coef = dot_tn(inverse, right)
    group[...] = dot_tn(full[y], coef)
    grad = group[pl.ds(pl.multiple_of(z * owned, 8), owned)]

    for d in ORDER[::-1]:
        copy(5, 0, "s", d, norms.at[down(section, d)], norms.at[down(section, d)]).wait_recv()
    squares = norms[0]
    for i in range(1, RING):
        squares += norms[i]
    clip = jnp.minimum(1.0, clip_limit / jnp.sqrt(squares))[0:1, 0:1]
    scaled = clip * grad
    new_first = beta_one * first_ref[...] + (1.0 - beta_one) * scaled
    new_second = beta_two * second_ref[...] + (1.0 - beta_two) * scaled * scaled
    adam_step = (
        new_first
        / (1.0 - beta_one**STEP)
        / (jnp.sqrt(new_second / (1.0 - beta_two**STEP)) + adam_epsilon)
    )
    new_master = master_ref[...] - learn_rate * adam_step
    new_first_ref[...] = new_first
    new_second_ref[...] = new_second
    new_master_ref[...] = new_master
    short = new_master.astype(BF16)
    gat_a[z] = short[:, 0:128]
    gat_b[y] = short[:, 64:192]
    for d in ORDER:
        send(6, 0, "z", d, gat_a.at[z], gat_a.at[z])
        send(6, 1, "y", d, gat_b.at[y], gat_b.at[y])
    for d in ORDER[::-1]:
        copy(6, 0, "z", d, gat_a.at[down(z, d)], gat_a.at[down(z, d)]).wait_recv()
        copy(6, 1, "y", d, gat_b.at[down(y, d)], gat_b.at[down(y, d)]).wait_recv()
    rows = g_ref.shape[0] // 2
    mine = pl.ds(pl.multiple_of(y * width, 128), width)
    out_ref[0:rows, mine] = gat_a[...].reshape(width, 128).T[0:rows]
    tail_b[z] = gat_b[...]
    for d in ORDER:
        here = out_ref.at[pl.ds(0, rows), mine]
        send(7, 0, "y", d, here, here)
        send(7, 1, "z", d, tail_b.at[z], tail_b.at[z])

    high, low, _ = three_parts(coef)
    left = jnp.concatenate([high, high, low], axis=0)
    for j in range(RING):
        cols = pl.ds(j * width, width)
        high, low, _ = three_parts(full[j])
        approx = lax.dot_general(
            left, jnp.concatenate([high, low, high], axis=0), (((0,), (0,)), ((), ())),
            preferred_element_type=F32,
        )
        combined = g_ref[:, cols].astype(F32) + e_ref[:, cols].astype(F32)
        err_ref[:, cols] = (combined - approx).astype(BF16)

    for d in ORDER[::-1]:
        copy(7, 1, "z", d, tail_b.at[down(z, d)], tail_b.at[down(z, d)]).wait_recv()
    for j in range(RING):
        block = tail_b[:, j].reshape(width, 128)
        out_ref[rows:, j * width : (j + 1) * width] = block.T[128 - rows :]
    for d in ORDER[::-1]:
        there = out_ref.at[pl.ds(0, rows), pl.ds(pl.multiple_of(down(y, d) * width, 128), width)]
        copy(7, 0, "y", d, there, there).wait_recv()
    for c in started:
        c.wait_send()


def per_device(gradients, error_buffers, initial_q, master, first_moment, second_moment):
    rows, cols = gradients.shape[2:]
    rank = initial_q.shape[2]
    owned = master.shape[2]
    half = rank // 2
    width = cols // RING
    vmem = pl.BlockSpec(memory_space=pltpu.VMEM)
    outs = pl.pallas_call(
        step_kernel,
        name="relay_step",
        out_shape=(
            jax.ShapeDtypeStruct((rows, cols), BF16),
            jax.ShapeDtypeStruct((rank, rows), F32),
            jax.ShapeDtypeStruct((owned, rows), F32),
            jax.ShapeDtypeStruct((owned, rows), F32),
            jax.ShapeDtypeStruct((owned, rows), F32),
            jax.ShapeDtypeStruct((rows, cols), BF16),
        ),
        in_specs=[vmem] * 6,
        out_specs=(vmem,) * 6,
        scratch_shapes=[
            pltpu.VMEM((RING, rank, width), F32),
            pltpu.VMEM((RING - 1, half, width), F32),
            pltpu.VMEM((RING - 1, half, width), F32),
            pltpu.VMEM((RING, half, width), F32),
            pltpu.VMEM((RING, half, width), F32),
            pltpu.VMEM((RING, rank, width), F32),
            pltpu.VMEM((48, 128), F32),
            pltpu.VMEM((RING, 24, 128), F32),
            pltpu.VMEM((RING, 24, 128), F32),
            pltpu.VMEM((RING, 24, 128), F32),
            pltpu.VMEM((RING, 24, 128), F32),
            pltpu.VMEM((8, 128), F32),
            pltpu.VMEM((RING, 8, 128), F32),
            pltpu.VMEM((width, rows), F32),
            pltpu.VMEM((owned, 128), BF16),
            pltpu.VMEM((owned, 128), BF16),
            pltpu.VMEM((RING, owned, 128), BF16),
            pltpu.VMEM((RING, owned, 128), BF16),
            pltpu.VMEM((rows // 2, width), BF16),
            pltpu.VMEM((RING, RING, owned, 128), BF16),
            pltpu.SemaphoreType.DMA((8, 2, RING)),
            pltpu.SemaphoreType.DMA((8, 2, RING)),
        ],
        compiler_params=pltpu.CompilerParams(
            collective_id=0, has_side_effects=True, vmem_limit_bytes=40 << 20
        ),
    )(
        gradients[0, 0],
        error_buffers[0, 0],
        initial_q[0].T,
        master[0].T,
        first_moment[0].T,
        second_moment[0].T,
    )
    new_errors, right, new_master, new_first, new_second, gathered = outs
    return (
        new_errors[None, None],
        right.T[None],
        new_master.T[None],
        new_first.T[None],
        new_second.T[None],
        gathered[None],
    )


def solution(mesh):
    placed = (
        P("section", "dp", None, None),
        P("section", "dp", None, None),
        P("section", None, None),
        P("section", None, "dp"),
        P("section", None, "dp"),
        P("section", None, "dp"),
    )
    return jax.shard_map(
        per_device,
        mesh=mesh,
        in_specs=placed,
        out_specs=(
            P("section", "dp", None, None),
            P("section", None, None),
            P("section", None, "dp"),
            P("section", None, "dp"),
            P("section", None, "dp"),
            P("section", None, None),
        ),
        check_vma=False,
    )
```

time: 645 us -> 88.4 us (0.14)
  blocking collectives: 375 us -> 0 us
  waiting for transfers between devices: 227 us -> 0 us
  Pallas kernels: 0 us -> 77.1 us
  between operations: 14.8 us -> 0.66 us
  matrix products: 13.7 us -> 0 us
  other arithmetic: 8.01 us -> 0 us
  local copies, waits for them, and re-layouts: 3.28 us -> 10.2 us
    psum x2 -> x0, blocking collectives: 375 us -> none  [the longest x1 222 us: per_device(): right_factor = lax.psum(local_right, 'dp') / replicas]
    psum x1 -> x0, waiting for transfers between devices: 156 us -> none  [per_device(): projected = lax.psum(local_power, 'dp')]
    pallas_call x0 -> x1, Pallas kernels: none -> 77.1 us  [per_device(): pl.pallas_call(step_kernel, name='relay_step', out_shape=(jax.ShapeDtypeS...]
    all_gather x1 -> x0, waiting for transfers between devices: 70.5 us -> none  [per_device(): lax.all_gather(new_master.astype(jnp.bfloat16), 'dp', axis=1, tiled=True)]
    dot_general x5 -> x0, matrix products: 12.1 us -> none  [the longest x1 4.28 us: per_device(): local_power = jnp.dot(combined.T, start_q, precision=lax.Precision.HIGHEST)]
    unnamed x13 -> x18, local copies, waits for them, and re-layouts: 3.21 us -> 10.2 us
    another operation x5 -> x0, other arithmetic: 6.68 us -> none  [the longest x3 3.6 us: basis_from(): cholesky_factor = jnp.linalg.cholesky(gram_matrix)]
  transfers between devices with their start and end apart: 2 -> 0, of which waited for: 2 -> 0; matrix products, arithmetic and copies ran while one was open for 1% -> 0% of each run, Pallas kernels for 0% -> 0%
where the time goes in v1:
time: 88.4 us; the launch traced here: 88 us
  Pallas kernels  77.1 us (87%)
  local copies, waits for them, and re-layouts  10.2 us (12%)
    pallas_call x1, Pallas kernels, per_device(): pl.pallas_call(step_kernel, name='relay_step', out_shape=(jax.ShapeDtypeS...  77.1 us
    unnamed x18, local copies, waits for them, and re-layouts  10.2 us

profile of v1, /device:TPU:1, one launch (start us, length us, event | category | flops | bytes accessed | tf_op | source)
XLA Modules:
  0.0 88.0 jit_solution(1627588314503336722)
XLA Ops:
  0.6 0.0 copy-start
  0.6 1.3 %copy-done = bf16[1,1,192,3072]{3,2,1,0:T(8,128)(2,1)S(1)} copy-done((bf16[1,1,192,3072]{3,2,1,0:T(8,128)(2,1)S(1)}, bf16[1,1,192,3072]{3,2,1,0:T(8,128)(2,1)}, u32[]{:S(2)}) %copy-start) | copy-done | bytes 1179672
  1.9 0.0 copy-start.1
  1.9 1.3 %copy-done.1 = bf16[1,1,192,3072]{3,2,1,0:T(8,128)(2,1)S(1)} copy-done((bf16[1,1,192,3072]{3,2,1,0:T(8,128)(2,1)S(1)}, bf16[1,1,192,3072]{3,2,1,0:T(8,128)(2,1)}, u32[]{:S(2)}) %copy-start.1) | copy-done | bytes 1179672
  3.2 0.0 copy-start.2
  3.2 0.8 copy-done.2
  4.0 0.0 copy-start.3
  4.0 0.8 copy-done.3
  4.8 0.0 copy-start.4
  4.8 0.8 copy-done.4
  5.6 0.0 copy-start.5
  5.6 0.8 copy-done.5
  6.3 77.1 %relay_step.1 = (bf16[192,3072]{1,0:T(8,128)(2,1)S(1)}, f32[32,192]{1,0:T(8,128)S(1)}, f32[48,192]{1,0:T(8,128)S(1)}, f32[48,192]{1,0:T(8,128)S(1)}, f32[48,192]...) custom-call(bf16[192,3072]{1,0:T(8,128)(2,1)S(1)} %bitcast.28, bf16[192,3072]{1,0:T(8,128)(2,1)S(1)} %bitcast.29, ...), custom_call_target="tpu_custom_call" | custom-call | tf_op jit(solution)/shard_map/relay_step/pallas_call | solution.py:282
  83.5 1.0 %copy.18 = bf16[1,1,192,3072]{3,2,1,0:T(8,128)(2,1)} copy(bf16[1,1,192,3072]{3,2,1,0:T(8,128)(2,1)S(1)} %bitcast.31) | data formatting | bytes 2359296
  84.5 0.6 copy.19
  85.1 0.6 copy.20
  85.7 0.6 copy.21
  86.3 0.6 copy.22
  87.0 1.0 %copy.23 = bf16[1,192,3072]{2,1,0:T(8,128)(2,1)} copy(bf16[1,192,3072]{2,1,0:T(8,128)(2,1)S(1)} %bitcast.30) | data formatting | bytes 2359296
Async XLA Ops:
  0.6 1.3 %copy-start = (bf16[1,1,192,3072]{3,2,1,0:T(8,128)(2,1)S(1)}, bf16[1,1,192,3072]{3,2,1,0:T(8,128)(2,1)}, u32[]{:S(2)}) copy-start(bf16[1,1,192,3072]{3,2,1,0:T(8,128)(2,1)} %param.6) | copy-start | bytes 3538948
  1.9 1.3 %copy-start.1 = (bf16[1,1,192,3072]{3,2,1,0:T(8,128)(2,1)S(1)}, bf16[1,1,192,3072]{3,2,1,0:T(8,128)(2,1)}, u32[]{:S(2)}) copy-start(bf16[1,1,192,3072]{3,2,1,0:T(8,128)(2,1)} %param.7) | copy-start | bytes 3538948
  3.2 0.8 copy-start.2
  4.0 0.8 copy-start.3
  4.8 0.8 copy-start.4
  5.6 0.8 copy-start.5

commit v2 on v1

v2 whole, which is shorter than its diff:
```python
import functools

import jax
import jax.numpy as jnp
from jax import lax
from jax.experimental import pallas as pl
from jax.experimental.pallas import tpu as pltpu
from jax.sharding import PartitionSpec as P

STEP = 10


beta_one = 0.9
beta_two = 0.999
adam_epsilon = 1e-08
learn_rate = 0.02
clip_limit = 16.0

RING = 8
ORDER = (4, 3, 5, 2, 6, 1, 7)
MESH = pl.DeviceIdType.MESH
HIGH = lax.Precision.HIGHEST
F32 = jnp.float32
BF16 = jnp.bfloat16


def dot_nn(a, b):
    return lax.dot_general(a, b, (((1,), (0,)), ((), ())), precision=HIGH, preferred_element_type=F32)


def dot_tn(a, b):
    return lax.dot_general(a, b, (((0,), (0,)), ((), ())), precision=HIGH, preferred_element_type=F32)


def dot_nt(a, b):
    return lax.dot_general(a, b, (((1,), (1,)), ((), ())), precision=HIGH, preferred_element_type=F32)


def three_parts(value):
    high = value.astype(BF16)
    rest = value - high.astype(F32)
    middle = rest.astype(BF16)
    low = (rest - middle.astype(F32)).astype(BF16)
    return high, middle, low


def widen(gram):
    rank = gram.shape[0]
    rows = lax.broadcasted_iota(jnp.int32, (rank, 128), 0)
    lanes = lax.broadcasted_iota(jnp.int32, (rank, 128), 1)
    identity = jnp.where(lanes == rows + rank, 1.0, 0.0).astype(F32)
    wide = jnp.concatenate([gram, jnp.zeros((rank, 128 - rank), F32)], axis=1) + identity
    return wide, jnp.ones((rank, 128), F32)


def eliminate(state, first, last):
    wide, pivots = state
    rank = wide.shape[0]
    rows = lax.broadcasted_iota(jnp.int32, (rank, 128), 0)
    for k in range(first, last):
        column = jnp.broadcast_to(wide[:, k : k + 1], (rank, 128))
        pivot = jnp.broadcast_to(column[k : k + 1, :], (rank, 128))
        row = jnp.broadcast_to(wide[k : k + 1, :], (rank, 128))
        pivots = jnp.where(rows == k, pivot, pivots)
        factor = jnp.where(rows > k, column / pivot, 0.0)
        wide = wide - factor * row
    return wide, pivots


def step_kernel(
    g_hbm, e_hbm, q_hbm, master_hbm, first_hbm, second_hbm,
    err_ref, right_ref, new_master_ref, new_first_ref, new_second_ref, out_ref,
    g_ref, e_ref, q_ref, states, local, red_a, red_b, sum_a, sum_b, full, fold_a, fold_b, next_a, next_b,
    norms, pre_a, pre_b, grad_a, grad_b, tail_b, loads, ss, rs,
):
    section = lax.axis_index("section")
    dp = lax.axis_index("dp")
    y = lax.div(dp, RING)
    z = lax.rem(dp, RING)
    replicas = RING * RING
    rank = q_ref.shape[0]
    half = rank // 2
    width = g_ref.shape[1] // RING
    owned = master_hbm.shape[0]
    rows = g_ref.shape[0] // 2

    def up(i, d):
        return lax.rem(i + d, RING)

    def down(i, d):
        return lax.rem(i + RING - d, RING)

    def peer(axis, d):
        if axis == "z":
            return (section, y * RING + up(z, d))
        if axis == "y":
            return (section, up(y, d) * RING + z)
        return (up(section, d), dp)

    def remote(phase, lane, sem, axis, d, src, dst):
        return pltpu.make_async_remote_copy(
            src_ref=src, dst_ref=dst, send_sem=ss.at[phase, lane, sem], recv_sem=rs.at[phase, lane, sem],
            device_id=peer(axis, d), device_id_type=MESH,
        )

    def copy(phase, lane, axis, d, src, dst):
        return remote(phase, lane, d, axis, d, src, dst)

    started = []

    def send(*args):
        c = copy(*args)
        c.start()
        started.append(c)

    barrier = pltpu.get_barrier_semaphore()
    for axis in ("z", "y", "s"):
        for d in range(1, RING):
            pl.semaphore_signal(barrier, 1, device_id=peer(axis, d), device_id_type=MESH)

    sources = [(q_hbm, q_ref), (g_hbm, g_ref), (e_hbm, e_ref)]
    sources += [(x, states.at[i]) for i, x in enumerate((first_hbm, second_hbm, master_hbm))]
    fetch = [pltpu.make_async_copy(x, v, loads.at[i]) for i, (x, v) in enumerate(sources)]
    for c in fetch:
        c.start()
    for c in fetch[:3]:
        c.wait()

    parts = jnp.concatenate(three_parts(q_ref[...]), axis=0)
    for j in range(RING):
        cols = pl.ds(j * width, width)
        term = jnp.dot(parts, g_ref[:, cols], preferred_element_type=F32)
        term += jnp.dot(parts, e_ref[:, cols], preferred_element_type=F32)
        local[j] = term[:rank] + term[rank : 2 * rank] + term[2 * rank :]
    for c in fetch[3:]:
        c.wait()
    for i in range(3):
        value = states[i]
        pre_a[z, i] = value[:, :128]
        pre_b[y, i] = jnp.concatenate([value[:, rows:], value[:, : 128 - rows]], axis=1)

    pl.semaphore_wait(barrier, 3 * (RING - 1))

    def state_copy(lane, step, way):
        axis, place, buf = (("z", z, pre_a), ("y", y, pre_b))[lane]
        block = down(place, step - 1) if way == 0 else up(place, step - 1)
        view = buf.at[block]
        if step == RING // 2:
            part = owned // 2
            view = buf.at[block, :, pl.ds(part * way, part)]
        return remote(6, lane, way * 4 + step - 1, axis, 1 if way == 0 else RING - 1, view, view)

    def state_landed(lane, step, way):
        axis, place, buf = (("z", z, pre_a), ("y", y, pre_b))[lane]
        block = down(place, step) if way == 0 else up(place, step)
        view = buf.at[block]
        if step == RING // 2:
            part = owned // 2
            view = buf.at[block, :, pl.ds(part * way, part)]
        return remote(6, lane, way * 4 + step - 1, axis, 1 if way == 0 else RING - 1, view, view)

    def state_step(step):
        for lane in range(2):
            for way in range(2):
                if step > 1:
                    state_landed(lane, step - 1, way).wait_recv()
                if step <= RING // 2:
                    c = state_copy(lane, step, way)
                    c.start()
                    started.append(c)

    for d in ORDER:
        send(0, 0, "z", d, local.at[up(z, d), pl.ds(0, half)], red_a.at[d - 1])
        send(0, 1, "y", d, local.at[up(y, d), pl.ds(half, half)], red_b.at[d - 1])
    state_step(1)
    total_a = local[z, 0:half]
    total_b = local[y, half:rank]
    for d in ORDER[::-1]:
        copy(0, 0, "z", d, red_a.at[d - 1], red_a.at[d - 1]).wait_recv()
        total_a += red_a[d - 1]
        copy(0, 1, "y", d, red_b.at[d - 1], red_b.at[d - 1]).wait_recv()
        total_b += red_b[d - 1]
    sum_a[y] = total_a
    sum_b[z] = total_b
    for d in ORDER:
        send(1, 0, "y", d, sum_a.at[y], sum_a.at[y])
        send(1, 1, "z", d, sum_b.at[z], sum_b.at[z])
    state_step(2)
    for d in ORDER[::-1]:
        copy(1, 0, "y", d, sum_a.at[down(y, d)], sum_a.at[down(y, d)]).wait_recv()
        copy(1, 1, "z", d, sum_b.at[down(z, d)], sum_b.at[down(z, d)]).wait_recv()
    total_a = sum_a[0]
    total_b = sum_b[0]
    for i in range(1, RING):
        total_a += sum_a[i]
        total_b += sum_b[i]
    full[z, 0:half] = total_a
    full[y, half:rank] = total_b
    for d in ORDER:
        send(2, 0, "z", d, full.at[z, pl.ds(0, half)], full.at[z, pl.ds(0, half)])
        send(2, 1, "y", d, full.at[y, pl.ds(half, half)], full.at[y, pl.ds(half, half)])
    state_step(3)
    for d in ORDER[::-1]:
        src_z, src_y = down(z, d), down(y, d)
        copy(2, 0, "z", d, full.at[src_z, pl.ds(0, half)], full.at[src_z, pl.ds(0, half)]).wait_recv()
        copy(2, 1, "y", d, full.at[src_y, pl.ds(half, half)], full.at[src_y, pl.ds(half, half)]).wait_recv()

    right = jnp.zeros((3 * rank, g_ref.shape[0]), F32)
    for j in range(RING):
        cols = pl.ds(j * width, width)
        parts = jnp.concatenate(three_parts(full[j]), axis=0)
        for source in (g_ref, e_ref):
            right += lax.dot_general(
                parts, source[:, cols], (((1,), (1,)), ((), ())), preferred_element_type=F32
            )
    right = right[:rank] + right[rank : 2 * rank] + right[2 * rank :]
    rest = jnp.concatenate([right[:half, 128:192], right[half:, 128:192]], axis=1)
    fold_a[z, 0:16] = right[:half, :128]
    fold_a[z, 16:24] = rest[:8]
    fold_b[y, 0:16] = right[half:, :128]
    fold_b[y, 16:24] = rest[8:]
    for d in ORDER:
        send(3, 0, "z", d, fold_a.at[z], fold_a.at[z])
        send(3, 1, "y", d, fold_b.at[y], fold_b.at[y])
    state_step(4)

    gram = jnp.zeros((rank, rank), F32)
    for j in range(RING):
        gram += dot_nt(full[j], full[j])
    state = eliminate(widen(gram), 0, rank // 2)

    for d in ORDER[::-1]:
        copy(3, 0, "z", d, fold_a.at[down(z, d)], fold_a.at[down(z, d)]).wait_recv()
        copy(3, 1, "y", d, fold_b.at[down(y, d)], fold_b.at[down(y, d)]).wait_recv()
    total_a = fold_a[0]
    total_b = fold_b[0]
    for i in range(1, RING):
        total_a += fold_a[i]
        total_b += fold_b[i]
    next_a[y] = total_a
    next_b[z] = total_b
    for d in ORDER:
        send(4, 0, "y", d, next_a.at[y], next_a.at[y])
        send(4, 1, "z", d, next_b.at[z], next_b.at[z])

    wide, pivots = eliminate(state, rank // 2, rank)
    inverse = (wide * lax.rsqrt(pivots))[:, rank : 2 * rank]
    from_col = lax.broadcasted_iota(jnp.int32, (width, width), 0)
    to_col = lax.broadcasted_iota(jnp.int32, (width, width), 1)
    picked = jnp.zeros((3 * rank, width), F32)
    for i in range(RING):
        chosen = jnp.where(
            (from_col - owned * z == to_col - owned * i) & (to_col >= owned * i) & (to_col < owned * (i + 1)),
            1.0, 0.0,
        ).astype(BF16)
        parts = jnp.concatenate(three_parts(full[i]), axis=0)
        picked += jnp.dot(parts, chosen, preferred_element_type=F32)
    picked = picked[:rank] + picked[rank : 2 * rank] + picked[2 * rank :]

    for d in ORDER[::-1]:
        copy(4, 0, "y", d, next_a.at[down(y, d)], next_a.at[down(y, d)]).wait_recv()
        copy(4, 1, "z", d, next_b.at[down(z, d)], next_b.at[down(z, d)]).wait_recv()
    total_a = next_a[0]
    total_b = next_b[0]
    for i in range(1, RING):
        total_a += next_a[i]
        total_b += next_b[i]
    rest = jnp.concatenate([total_a[16:24], total_b[16:24]], axis=0)
    top = jnp.concatenate([total_a[0:16], total_b[0:16]], axis=0)
    rest = jnp.concatenate([rest[:, :64], rest[:, 64:]], axis=0)
    right = jnp.concatenate([top, rest], axis=1)
    right = dot_nn(inverse, right) * (1.0 / replicas)
    squares = jnp.sum(right * right, keepdims=True)
    norms[section] = jnp.broadcast_to(squares, (8, 128))
    for d in ORDER:
        send(5, 0, "s", d, norms.at[section], norms.at[section])
    right_ref[...] = right
    state_step(5)

    coef = dot_tn(inverse, right)
    grad_a[...] = dot_tn(full[y], coef[:, :128])
    grad_b[...] = dot_tn(picked, jnp.concatenate([coef[:, rows:], coef[:, : 128 - rows]], axis=1))
    high, low, _ = three_parts(coef)
    left = jnp.concatenate([high, high, low], axis=0)
    for j in range(RING):
        cols = pl.ds(j * width, width)
        high, low, _ = three_parts(full[j])
        approx = lax.dot_general(
            left, jnp.concatenate([high, low, high], axis=0), (((0,), (0,)), ((), ())),
            preferred_element_type=F32,
        )
        combined = g_ref[:, cols].astype(F32) + e_ref[:, cols].astype(F32)
        err_ref[:, cols] = (combined - approx).astype(BF16)

    for d in ORDER[::-1]:
        copy(5, 0, "s", d, norms.at[down(section, d)], norms.at[down(section, d)]).wait_recv()
    squares = norms[0]
    for i in range(1, RING):
        squares += norms[i]
    clip = jnp.minimum(1.0, clip_limit / jnp.sqrt(squares))[0:1, 0:1]

    def update(grad, first, second, master):
        scaled = clip * grad
        new_first = beta_one * first + (1.0 - beta_one) * scaled
        new_second = beta_two * second + (1.0 - beta_two) * scaled * scaled
        adam_step = (
            new_first
            / (1.0 - beta_one**STEP)
            / (jnp.sqrt(new_second / (1.0 - beta_two**STEP)) + adam_epsilon)
        )
        return master - learn_rate * adam_step, new_first, new_second

    def group_update(grad, buf):
        first, second, master = (buf[:, i].reshape(width, 128) for i in range(3))
        return update(grad, first, second, master)[0]

    mine = pl.ds(pl.multiple_of(y * width, 128), width)
    out_ref[0:rows, mine] = group_update(grad_a[...], pre_a).astype(BF16).T[0:rows]

    def weight_copy(lane, sem, here, there):
        axis, place = (("y", y), ("z", z))[lane]
        part, d = (
            (None, 2), (None, RING - 2), (None, 1), (None, RING - 1),
            (0, 2), (None, 1), (1, RING - 2), (None, RING - 1),
        )[sem]

        def view(block):
            if lane == 0:
                lanes = pl.ds(pl.multiple_of(block * width, 128), width)
                if part is None:
                    return out_ref.at[pl.ds(0, rows), lanes]
                return out_ref.at[pl.ds(part * (rows // 2), rows // 2), lanes]
            if part is None:
                return tail_b.at[block]
            return tail_b.at[block, pl.ds(3 * part, 3)]

        return remote(7, lane, sem, axis, d, view(here), view(there))

    def weight_start(lane, sem):
        place = (y, z)[lane]
        block = (place, place, place, place, down(place, 2), down(place, 2), up(place, 2), up(place, 2))[sem]
        c = weight_copy(lane, sem, block, block)
        c.start()
        started.append(c)

    def weight_landed(lane, sem):
        place = (y, z)[lane]
        block = (
            down(place, 2), up(place, 2), down(place, 1), up(place, 1),
            down(place, 4), down(place, 3), up(place, 4), up(place, 3),
        )[sem]
        weight_copy(lane, sem, block, block).wait_recv()

    for sem in range(4):
        weight_start(0, sem)
    tail = group_update(grad_b[...], pre_b)
    lanes = lax.broadcasted_iota(jnp.int32, (owned, 128), 1)
    for i in range(6):
        other = tail[(6 + i % 2) * owned : (7 + i % 2) * owned]
        shift = rows - 32 * (i // 2)
        other = jnp.concatenate([other[:, 128 - shift :], other[:, : 128 - shift]], axis=1)
        tail_b[z, i] = jnp.where(lanes < rows, tail[i * owned : (i + 1) * owned], other).astype(BF16)
    for sem in range(4):
        weight_start(1, sem)

    own_a = grad_a[pl.ds(pl.multiple_of(z * owned, 8), owned)]
    own_b = grad_b[pl.ds(pl.multiple_of(y * owned, 8), owned)]
    grad = jnp.concatenate([own_a[:, :rows], own_b[:, :rows]], axis=1)
    new_master, new_first, new_second = update(grad, states[0], states[1], states[2])
    new_master_ref[...] = new_master
    new_first_ref[...] = new_first
    new_second_ref[...] = new_second

    for sem in (0, 1):
        for lane in (0, 1):
            weight_landed(lane, sem)
            weight_start(lane, 4 + 2 * sem)
            weight_start(lane, 5 + 2 * sem)
    for sem in range(2, 8):
        weight_landed(1, sem)
    for i in range(6):
        block = tail_b[:, i].reshape(width, 128).T
        out_ref[rows:, i * width : (i + 1) * width] = block[:rows]
        first_row = rows + 32 * (i // 2)
        first_col = (6 + i % 2) * width
        out_ref[first_row : first_row + 32, first_col : first_col + width] = block[rows:]
    for sem in range(2, 8):
        weight_landed(0, sem)
    for c in started:
        c.wait_send()


def finish_kernel(*refs):
    sources, targets, sems = refs[:6], refs[6:12], refs[12]
    copies = [pltpu.make_async_copy(s, t, sems.at[i]) for i, (s, t) in enumerate(zip(sources, targets))]
    for c in copies:
        c.start()
    for c in copies:
        c.wait()


def per_device(gradients, error_buffers, initial_q, master, first_moment, second_moment):
    rows, cols = gradients.shape[2:]
    rank = initial_q.shape[2]
    owned = master.shape[2]
    half = rank // 2
    width = cols // RING
    vmem = pl.BlockSpec(memory_space=pltpu.VMEM)
    hbm = pl.BlockSpec(memory_space=pltpu.HBM)
    shapes = (
        jax.ShapeDtypeStruct((rows, cols), BF16),
        jax.ShapeDtypeStruct((rank, rows), F32),
        jax.ShapeDtypeStruct((owned, rows), F32),
        jax.ShapeDtypeStruct((owned, rows), F32),
        jax.ShapeDtypeStruct((owned, rows), F32),
        jax.ShapeDtypeStruct((rows, cols), BF16),
    )
    operands = (gradients[0, 0], error_buffers[0, 0], initial_q[0].T)
    operands += (master[0].T, first_moment[0].T, second_moment[0].T)
    outs = pl.pallas_call(
        step_kernel,
        name="relay_step",
        out_shape=tuple(pltpu.VMEM(x.shape, x.dtype) for x in shapes),
        in_specs=[hbm] * 6,
        out_specs=(vmem,) * 6,
        scratch_shapes=[
            pltpu.VMEM((rows, cols), BF16),
            pltpu.VMEM((rows, cols), BF16),
            pltpu.VMEM((rank, rows), F32),
            pltpu.VMEM((3, owned, rows), F32),
            pltpu.VMEM((RING, rank, width), F32),
            pltpu.VMEM((RING - 1, half, width), F32),
            pltpu.VMEM((RING - 1, half, width), F32),
            pltpu.VMEM((RING, half, width), F32),
            pltpu.VMEM((RING, half, width), F32),
            pltpu.VMEM((RING, rank, width), F32),
            pltpu.VMEM((RING, 24, 128), F32),
            pltpu.VMEM((RING, 24, 128), F32),
            pltpu.VMEM((RING, 24, 128), F32),
            pltpu.VMEM((RING, 24, 128), F32),
            pltpu.VMEM((RING, 8, 128), F32),
            pltpu.VMEM((RING, 3, owned, 128), F32),
            pltpu.VMEM((RING, 3, owned, 128), F32),
            pltpu.VMEM((width, 128), F32),
            pltpu.VMEM((width, 128), F32),
            pltpu.VMEM((RING, 6, owned, 128), BF16),
            pltpu.SemaphoreType.DMA((6,)),
            pltpu.SemaphoreType.DMA((8, 2, RING)),
            pltpu.SemaphoreType.DMA((8, 2, RING)),
        ],
        compiler_params=pltpu.CompilerParams(
            collective_id=0, has_side_effects=True, vmem_limit_bytes=40 << 20
        ),
    )(*(pltpu.with_memory_space_constraint(x, pltpu.HBM) for x in operands))
    outs = pl.pallas_call(
        finish_kernel,
        name="finish",
        out_shape=shapes,
        in_specs=[vmem] * 6,
        out_specs=(hbm,) * 6,
        scratch_shapes=[pltpu.SemaphoreType.DMA((6,))],
    )(*(pltpu.with_memory_space_constraint(x, pltpu.VMEM) for x in outs))
    new_errors, right, new_master, new_first, new_second, gathered = outs
    return (
        new_errors[None, None],
        right.T[None],
        new_master.T[None],
        new_first.T[None],
        new_second.T[None],
        gathered[None],
    )


def solution(mesh):
    placed = (
        P("section", "dp", None, None),
        P("section", "dp", None, None),
        P("section", None, None),
        P("section", None, "dp"),
        P("section", None, "dp"),
        P("section", None, "dp"),
    )
    return jax.shard_map(
        per_device,
        mesh=mesh,
        in_specs=placed,
        out_specs=(
            P("section", "dp", None, None),
            P("section", None, None),
            P("section", None, "dp"),
            P("section", None, "dp"),
            P("section", None, "dp"),
            P("section", None, None),
        ),
        check_vma=False,
    )
```

time: 88.4 us -> 66 us (0.75)
  Pallas kernels: 77.1 us -> 64.5 us
  local copies, waits for them, and re-layouts: 10.2 us -> 0 us
    pallas_call x1 -> x2, Pallas kernels: 77.1 us -> 64.5 us  [the longest x1 63 us: per_device(): pl.pallas_call(step_kernel, name='relay_step', out_shape=tuple((pltpu.VME...]
    unnamed x18 -> x0, local copies, waits for them, and re-layouts: 10.2 us -> none
where the time goes in v2:
time: 66 us; the launch traced here: 65.1 us
  Pallas kernels  64.5 us (98%)
    pallas_call x1, Pallas kernels, per_device(): pl.pallas_call(step_kernel, name='relay_step', out_shape=tuple((pltpu.VME...  63 us
    pallas_call x1, Pallas kernels, per_device(): pl.pallas_call(finish_kernel, name='finish', out_shape=shapes, in_specs=[...  1.52 us

profile of v2, /device:TPU:1, one launch (start us, length us, event | category | flops | bytes accessed | tf_op | source)
XLA Modules:
  0.0 65.1 jit_solution(7713523752480362309)
XLA Ops:
  0.6 63.0 %relay_step.1 = (bf16[192,3072]{1,0:T(8,128)(2,1)S(1)}, f32[32,192]{1,0:T(8,128)S(1)}, f32[48,192]{1,0:T(8,128)S(1)}, f32[48,192]{1,0:T(8,128)S(1)}, f32[48,192]...) custom-call(bf16[192,3072]{1,0:T(8,128)(2,1)} %bitcast.28, bf16[192,3072]{1,0:T(8,128)(2,1)} %bitcast.29, f32[32,192]{1,0:T(8,128)} %bitcast.33, ...), custom_call_target="tpu_custom_call" | custom-call | tf_op jit(solution)/shard_map/relay_step/pallas_call | solution.py:420
  63.6 1.5 %finish.1 = (bf16[192,3072]{1,0:T(8,128)(2,1)}, f32[32,192]{1,0:T(8,128)}, f32[48,192]{1,0:T(8,128)}, f32[48,192]{1,0:T(8,128)}, f32[48,192]{1,0:T(8,128)}, /*index=5*/bf16[192,3072]{1,0:T(8,128)(2,1)}) custom-call(bf16[192,3072]{1,0:T(8,128)(2,1)S(1)} %get-tuple-element.18.refs_0_, f32[32,192]{1,0:T(8,128)S(1)} %get-tuple-element.19.refs_1_, ...), custom_call_target="tpu_custom_call" | custom-call | tf_op jit(solution)/shard_map/finish/pallas_call | solution.py:455

commit v3 on v2

--- a/solution.py
+++ b/solution.py
@@ -103,8 +103,8 @@
             device_id=peer(axis, d), device_id_type=MESH,
         )
 
-    def copy(phase, lane, axis, d, src, dst):
-        return remote(phase, lane, d, axis, d, src, dst)
+    def copy(phase, lane, axis, d, src, dst, chunk=0):
+        return remote(phase, lane, d + RING * chunk, axis, d, src, dst)
 
     started = []
 
@@ -118,21 +118,26 @@
         for d in range(1, RING):
             pl.semaphore_signal(barrier, 1, device_id=peer(axis, d), device_id_type=MESH)
 
-    sources = [(q_hbm, q_ref), (g_hbm, g_ref), (e_hbm, e_ref)]
+    sources = [(q_hbm, q_ref)]
+    for i in range(2):
+        cols = pl.ds(i * (RING // 2) * width, (RING // 2) * width)
+        sources += [(g_hbm.at[:, cols], g_ref.at[:, cols]), (e_hbm.at[:, cols], e_ref.at[:, cols])]
     sources += [(x, states.at[i]) for i, x in enumerate((first_hbm, second_hbm, master_hbm))]
     fetch = [pltpu.make_async_copy(x, v, loads.at[i]) for i, (x, v) in enumerate(sources)]
     for c in fetch:
         c.start()
-    for c in fetch[:3]:
-        c.wait()
+    fetch[0].wait()
 
     parts = jnp.concatenate(three_parts(q_ref[...]), axis=0)
     for j in range(RING):
+        if j % (RING // 2) == 0:
+            for c in fetch[1 + j // 2 : 3 + j // 2]:
+                c.wait()
         cols = pl.ds(j * width, width)
         term = jnp.dot(parts, g_ref[:, cols], preferred_element_type=F32)
         term += jnp.dot(parts, e_ref[:, cols], preferred_element_type=F32)
         local[j] = term[:rank] + term[rank : 2 * rank] + term[2 * rank :]
-    for c in fetch[3:]:
+    for c in fetch[5:]:
         c.wait()
     for i in range(3):
         value = states[i]
@@ -169,50 +174,66 @@
                     c.start()
                     started.append(c)
 
-    for d in ORDER:
-        send(0, 0, "z", d, local.at[up(z, d), pl.ds(0, half)], red_a.at[d - 1])
-        send(0, 1, "y", d, local.at[up(y, d), pl.ds(half, half)], red_b.at[d - 1])
+    step = half // 2
+    chunks = range(2)
+
+    def near(c):
+        return pl.ds(c * step, step)
+
+    def far(c):
+        return pl.ds(half + c * step, step)
+
+    for c in chunks:
+        for d in ORDER:
+            send(0, 0, "z", d, local.at[up(z, d), near(c)], red_a.at[d - 1, near(c)], c)
+            send(0, 1, "y", d, local.at[up(y, d), far(c)], red_b.at[d - 1, near(c)], c)
     state_step(1)
-    total_a = local[z, 0:half]
-    total_b = local[y, half:rank]
-    for d in ORDER[::-1]:
-        copy(0, 0, "z", d, red_a.at[d - 1], red_a.at[d - 1]).wait_recv()
-        total_a += red_a[d - 1]
-        copy(0, 1, "y", d, red_b.at[d - 1], red_b.at[d - 1]).wait_recv()
-        total_b += red_b[d - 1]
-    sum_a[y] = total_a
-    sum_b[z] = total_b
-    for d in ORDER:
-        send(1, 0, "y", d, sum_a.at[y], sum_a.at[y])
-        send(1, 1, "z", d, sum_b.at[z], sum_b.at[z])
+    for c in chunks:
+        total_a = local[z, near(c)]
+        total_b = local[y, far(c)]
+        for d in ORDER[::-1]:
+            here = red_a.at[d - 1, near(c)]
+            copy(0, 0, "z", d, here, here, c).wait_recv()
+            total_a += here[...]
+            here = red_b.at[d - 1, near(c)]
+            copy(0, 1, "y", d, here, here, c).wait_recv()
+            total_b += here[...]
+        sum_a[y, near(c)] = total_a
+        sum_b[z, near(c)] = total_b
+        for d in ORDER:
+            send(1, 0, "y", d, sum_a.at[y, near(c)], sum_a.at[y, near(c)], c)
+            send(1, 1, "z", d, sum_b.at[z, near(c)], sum_b.at[z, near(c)], c)
     state_step(2)
-    for d in ORDER[::-1]:
-        copy(1, 0, "y", d, sum_a.at[down(y, d)], sum_a.at[down(y, d)]).wait_recv()
-        copy(1, 1, "z", d, sum_b.at[down(z, d)], sum_b.at[down(z, d)]).wait_recv()
-    total_a = sum_a[0]
-    total_b = sum_b[0]
-    for i in range(1, RING):
-        total_a += sum_a[i]
-        total_b += sum_b[i]
-    full[z, 0:half] = total_a
-    full[y, half:rank] = total_b
-    for d in ORDER:
-        send(2, 0, "z", d, full.at[z, pl.ds(0, half)], full.at[z, pl.ds(0, half)])
-        send(2, 1, "y", d, full.at[y, pl.ds(half, half)], full.at[y, pl.ds(half, half)])
+    for c in chunks:
+        for d in ORDER[::-1]:
+            here = sum_a.at[down(y, d), near(c)]
+            copy(1, 0, "y", d, here, here, c).wait_recv()
+            here = sum_b.at[down(z, d), near(c)]
+            copy(1, 1, "z", d, here, here, c).wait_recv()
+        total_a = sum_a[0, near(c)]
+        total_b = sum_b[0, near(c)]
+        for i in range(1, RING):
+            total_a += sum_a[i, near(c)]
+            total_b += sum_b[i, near(c)]
+        full[z, near(c)] = total_a
+        full[y, far(c)] = total_b
+        for d in ORDER:
+            send(2, 0, "z", d, full.at[z, near(c)], full.at[z, near(c)], c)
+            send(2, 1, "y", d, full.at[y, far(c)], full.at[y, far(c)], c)
     state_step(3)
-    for d in ORDER[::-1]:
-        src_z, src_y = down(z, d), down(y, d)
-        copy(2, 0, "z", d, full.at[src_z, pl.ds(0, half)], full.at[src_z, pl.ds(0, half)]).wait_recv()
-        copy(2, 1, "y", d, full.at[src_y, pl.ds(half, half)], full.at[src_y, pl.ds(half, half)]).wait_recv()
-
-    right = jnp.zeros((3 * rank, g_ref.shape[0]), F32)
-    for j in range(RING):
-        cols = pl.ds(j * width, width)
-        parts = jnp.concatenate(three_parts(full[j]), axis=0)
-        for source in (g_ref, e_ref):
-            right += lax.dot_general(
-                parts, source[:, cols], (((1,), (1,)), ((), ())), preferred_element_type=F32
-            )
+    for c in chunks:
+        for d in ORDER[::-1]:
+            here = full.at[down(z, d), near(c)]
+            copy(2, 0, "z", d, here, here, c).wait_recv()
+            here = full.at[down(y, d), far(c)]
+            copy(2, 1, "y", d, here, here, c).wait_recv()
+
+    whole = jnp.concatenate([full[j] for j in range(RING)], axis=1)
+    parts = jnp.concatenate(three_parts(whole), axis=0)
+    right = sum(
+        lax.dot_general(parts, source[...], (((1,), (1,)), ((), ())), preferred_element_type=F32)
+        for source in (g_ref, e_ref)
+    )
     right = right[:rank] + right[rank : 2 * rank] + right[2 * rank :]
     rest = jnp.concatenate([right[:half, 128:192], right[half:, 128:192]], axis=1)
     fold_a[z, 0:16] = right[:half, :128]
@@ -317,41 +338,31 @@
     mine = pl.ds(pl.multiple_of(y * width, 128), width)
     out_ref[0:rows, mine] = group_update(grad_a[...], pre_a).astype(BF16).T[0:rows]
 
-    def weight_copy(lane, sem, here, there):
+    hops = (
+        (2, 0, 0), (-2, 0, 0), (2, 0, 1), (-2, 0, 1), (1, 0, 0), (-1, 0, 0), (1, 0, 1), (-1, 0, 1),
+        (2, -2, 0), (1, -2, 0), (1, -2, 1), (-1, 2, 0), (-1, 2, 1), (-2, 2, 1),
+    )
+
+    def weight_copy(lane, sem, offset):
         axis, place = (("y", y), ("z", z))[lane]
-        part, d = (
-            (None, 2), (None, RING - 2), (None, 1), (None, RING - 1),
-            (0, 2), (None, 1), (1, RING - 2), (None, RING - 1),
-        )[sem]
-
-        def view(block):
-            if lane == 0:
-                lanes = pl.ds(pl.multiple_of(block * width, 128), width)
-                if part is None:
-                    return out_ref.at[pl.ds(0, rows), lanes]
-                return out_ref.at[pl.ds(part * (rows // 2), rows // 2), lanes]
-            if part is None:
-                return tail_b.at[block]
-            return tail_b.at[block, pl.ds(3 * part, 3)]
-
-        return remote(7, lane, sem, axis, d, view(here), view(there))
+        target, _, part = hops[sem]
+        block = up(place, offset % RING)
+        if lane == 0:
+            lanes = pl.ds(pl.multiple_of(block * width, 128), width)
+            view = out_ref.at[pl.ds(part * (rows // 2), rows // 2), lanes]
+        else:
+            view = tail_b.at[block, pl.ds(3 * part, 3)]
+        return remote(7, lane, sem, axis, target % RING, view, view)
 
     def weight_start(lane, sem):
-        place = (y, z)[lane]
-        block = (place, place, place, place, down(place, 2), down(place, 2), up(place, 2), up(place, 2))[sem]
-        c = weight_copy(lane, sem, block, block)
+        c = weight_copy(lane, sem, hops[sem][1])
         c.start()
         started.append(c)
 
     def weight_landed(lane, sem):
-        place = (y, z)[lane]
-        block = (
-            down(place, 2), up(place, 2), down(place, 1), up(place, 1),
-            down(place, 4), down(place, 3), up(place, 4), up(place, 3),
-        )[sem]
-        weight_copy(lane, sem, block, block).wait_recv()
-
-    for sem in range(4):
+        weight_copy(lane, sem, hops[sem][1] - hops[sem][0]).wait_recv()
+
+    for sem in range(8):
         weight_start(0, sem)
     tail = group_update(grad_b[...], pre_b)
     lanes = lax.broadcasted_iota(jnp.int32, (owned, 128), 1)
@@ -360,7 +371,7 @@
         shift = rows - 32 * (i // 2)
         other = jnp.concatenate([other[:, 128 - shift :], other[:, : 128 - shift]], axis=1)
         tail_b[z, i] = jnp.where(lanes < rows, tail[i * owned : (i + 1) * owned], other).astype(BF16)
-    for sem in range(4):
+    for sem in range(8):
         weight_start(1, sem)
 
     own_a = grad_a[pl.ds(pl.multiple_of(z * owned, 8), owned)]
@@ -371,12 +382,12 @@
     new_first_ref[...] = new_first
     new_second_ref[...] = new_second
 
-    for sem in (0, 1):
+    for sem, onward in ((0, (8, 9)), (1, (11,)), (2, (10,)), (3, (13, 12))):
         for lane in (0, 1):
             weight_landed(lane, sem)
-            weight_start(lane, 4 + 2 * sem)
-            weight_start(lane, 5 + 2 * sem)
-    for sem in range(2, 8):
+            for k in onward:
+                weight_start(lane, k)
+    for sem in range(4, 14):
         weight_landed(1, sem)
     for i in range(6):
         block = tail_b[:, i].reshape(width, 128).T
@@ -384,7 +395,7 @@
         first_row = rows + 32 * (i // 2)
         first_col = (6 + i % 2) * width
         out_ref[first_row : first_row + 32, first_col : first_col + width] = block[rows:]
-    for sem in range(2, 8):
+    for sem in range(4, 14):
         weight_landed(0, sem)
     for c in started:
         c.wait_send()
@@ -444,9 +455,9 @@
             pltpu.VMEM((width, 128), F32),
             pltpu.VMEM((width, 128), F32),
             pltpu.VMEM((RING, 6, owned, 128), BF16),
-            pltpu.SemaphoreType.DMA((6,)),
-            pltpu.SemaphoreType.DMA((8, 2, RING)),
-            pltpu.SemaphoreType.DMA((8, 2, RING)),
+            pltpu.SemaphoreType.DMA((8,)),
+            pltpu.SemaphoreType.DMA((8, 2, 2 * RING)),
+            pltpu.SemaphoreType.DMA((8, 2, 2 * RING)),
         ],
         compiler_params=pltpu.CompilerParams(
             collective_id=0, has_side_effects=True, vmem_limit_bytes=40 << 20

time: 66 us -> 67.5 us (1.023)
  Pallas kernels: 64.5 us -> 66.7 us
    pallas_call x1, Pallas kernels: 63 us -> 65.1 us  [per_device(): pl.pallas_call(step_kernel, name='relay_step', out_shape=tuple((pltpu.VME...]
where the time goes in v3:
time: 67.5 us; the launch traced here: 67.3 us
  Pallas kernels  66.7 us (99%)
    pallas_call x1, Pallas kernels, per_device(): pl.pallas_call(step_kernel, name='relay_step', out_shape=tuple((pltpu.VME...  65.1 us
    pallas_call x1, Pallas kernels, per_device(): pl.pallas_call(finish_kernel, name='finish', out_shape=shapes, in_specs=[...  1.52 us

profile of v3, /device:TPU:1, one launch (start us, length us, event | category | flops | bytes accessed | tf_op | source)
XLA Modules:
  0.0 67.3 jit_solution(16193805273867930581)
XLA Ops:
  0.6 65.1 %relay_step.1 = (bf16[192,3072]{1,0:T(8,128)(2,1)S(1)}, f32[32,192]{1,0:T(8,128)S(1)}, f32[48,192]{1,0:T(8,128)S(1)}, f32[48,192]{1,0:T(8,128)S(1)}, f32[48,192]...) custom-call(bf16[192,3072]{1,0:T(8,128)(2,1)} %bitcast.28, bf16[192,3072]{1,0:T(8,128)(2,1)} %bitcast.29, f32[32,192]{1,0:T(8,128)} %bitcast.33, ...), custom_call_target="tpu_custom_call" | custom-call | tf_op jit(solution)/shard_map/relay_step/pallas_call | solution.py:431
  65.8 1.5 %finish.1 = (bf16[192,3072]{1,0:T(8,128)(2,1)}, f32[32,192]{1,0:T(8,128)}, f32[48,192]{1,0:T(8,128)}, f32[48,192]{1,0:T(8,128)}, f32[48,192]{1,0:T(8,128)}, /*index=5*/bf16[192,3072]{1,0:T(8,128)(2,1)}) custom-call(bf16[192,3072]{1,0:T(8,128)(2,1)S(1)} %get-tuple-element.18.refs_0_, f32[32,192]{1,0:T(8,128)S(1)} %get-tuple-element.19.refs_1_, ...), custom_call_target="tpu_custom_call" | custom-call | tf_op jit(solution)/shard_map/finish/pallas_call | solution.py:466

commit v4 on v3

--- a/solution.py
+++ b/solution.py
@@ -17,6 +17,8 @@
 clip_limit = 16.0
 
 RING = 8
+CHUNKS = 2
+PIECES = 2
 ORDER = (4, 3, 5, 2, 6, 1, 7)
 MESH = pl.DeviceIdType.MESH
 HIGH = lax.Precision.HIGHEST
@@ -71,7 +73,7 @@
     g_hbm, e_hbm, q_hbm, master_hbm, first_hbm, second_hbm,
     err_ref, right_ref, new_master_ref, new_first_ref, new_second_ref, out_ref,
     g_ref, e_ref, q_ref, states, local, red_a, red_b, sum_a, sum_b, full, fold_a, fold_b, next_a, next_b,
-    norms, pre_a, pre_b, grad_a, grad_b, tail_b, loads, ss, rs,
+    norms, pre_a, pre_b, grad_a, grad_b, tail_b, loads, sent, landed, state_sent, state_came, weight_sent, weight_came,
 ):
     section = lax.axis_index("section")
     dp = lax.axis_index("dp")
@@ -97,21 +99,28 @@
             return (section, up(y, d) * RING + z)
         return (up(section, d), dp)
 
-    def remote(phase, lane, sem, axis, d, src, dst):
+    def remote(send_sem, recv_sem, axis, d, src, dst):
         return pltpu.make_async_remote_copy(
-            src_ref=src, dst_ref=dst, send_sem=ss.at[phase, lane, sem], recv_sem=rs.at[phase, lane, sem],
+            src_ref=src, dst_ref=dst, send_sem=send_sem, recv_sem=recv_sem,
             device_id=peer(axis, d), device_id_type=MESH,
         )
 
+    def slot(phase, lane, chunk):
+        return (2 * phase + lane) * CHUNKS + chunk if phase < 3 else 6 * CHUNKS + 2 * (phase - 3) + lane
+
     def copy(phase, lane, axis, d, src, dst, chunk=0):
-        return remote(phase, lane, d + RING * chunk, axis, d, src, dst)
-
-    started = []
+        k = slot(phase, lane, chunk)
+        return remote(sent.at[k], landed.at[k], axis, d, src, dst)
+
+    exchanges = []
 
     def send(*args):
-        c = copy(*args)
-        c.start()
-        started.append(c)
+        copy(*args).start()
+
+    def gathered(phase, lane, view, chunk=0):
+        c = copy(phase, lane, "z", 1, view, view, chunk)
+        c.wait_recv()
+        exchanges.append(c)
 
     barrier = pltpu.get_barrier_semaphore()
     for axis in ("z", "y", "s"):
@@ -153,7 +162,7 @@
         if step == RING // 2:
             part = owned // 2
             view = buf.at[block, :, pl.ds(part * way, part)]
-        return remote(6, lane, way * 4 + step - 1, axis, 1 if way == 0 else RING - 1, view, view)
+        return remote(state_sent.at[lane], state_came.at[lane, way * 4 + step - 1], axis, 1 if way == 0 else RING - 1, view, view)
 
     def state_landed(lane, step, way):
         axis, place, buf = (("z", z, pre_a), ("y", y, pre_b))[lane]
@@ -162,7 +171,7 @@
         if step == RING // 2:
             part = owned // 2
             view = buf.at[block, :, pl.ds(part * way, part)]
-        return remote(6, lane, way * 4 + step - 1, axis, 1 if way == 0 else RING - 1, view, view)
+        return remote(state_sent.at[lane], state_came.at[lane, way * 4 + step - 1], axis, 1 if way == 0 else RING - 1, view, view)
 
     def state_step(step):
         for lane in range(2):
@@ -170,12 +179,10 @@
                 if step > 1:
                     state_landed(lane, step - 1, way).wait_recv()
                 if step <= RING // 2:
-                    c = state_copy(lane, step, way)
-                    c.start()
-                    started.append(c)
-
-    step = half // 2
-    chunks = range(2)
+                    state_copy(lane, step, way).start()
+
+    step = half // CHUNKS
+    chunks = range(CHUNKS)
 
     def near(c):
         return pl.ds(c * step, step)
@@ -188,16 +195,15 @@
             send(0, 0, "z", d, local.at[up(z, d), near(c)], red_a.at[d - 1, near(c)], c)
             send(0, 1, "y", d, local.at[up(y, d), far(c)], red_b.at[d - 1, near(c)], c)
     state_step(1)
+    others = pl.ds(0, RING - 1)
     for c in chunks:
+        gathered(0, 0, red_a.at[:, near(c)], c)
+        gathered(0, 1, red_b.at[:, near(c)], c)
         total_a = local[z, near(c)]
         total_b = local[y, far(c)]
-        for d in ORDER[::-1]:
-            here = red_a.at[d - 1, near(c)]
-            copy(0, 0, "z", d, here, here, c).wait_recv()
-            total_a += here[...]
-            here = red_b.at[d - 1, near(c)]
-            copy(0, 1, "y", d, here, here, c).wait_recv()
-            total_b += here[...]
+        for i in range(RING - 1):
+            total_a += red_a[i, near(c)]
+            total_b += red_b[i, near(c)]
         sum_a[y, near(c)] = total_a
         sum_b[z, near(c)] = total_b
         for d in ORDER:
@@ -205,11 +211,8 @@
             send(1, 1, "z", d, sum_b.at[z, near(c)], sum_b.at[z, near(c)], c)
     state_step(2)
     for c in chunks:
-        for d in ORDER[::-1]:
-            here = sum_a.at[down(y, d), near(c)]
-            copy(1, 0, "y", d, here, here, c).wait_recv()
-            here = sum_b.at[down(z, d), near(c)]
-            copy(1, 1, "z", d, here, here, c).wait_recv()
+        gathered(1, 0, sum_a.at[others, near(c)], c)
+        gathered(1, 1, sum_b.at[others, near(c)], c)
         total_a = sum_a[0, near(c)]
         total_b = sum_b[0, near(c)]
         for i in range(1, RING):
@@ -222,11 +225,8 @@
             send(2, 1, "y", d, full.at[y, far(c)], full.at[y, far(c)], c)
     state_step(3)
     for c in chunks:
-        for d in ORDER[::-1]:
-            here = full.at[down(z, d), near(c)]
-            copy(2, 0, "z", d, here, here, c).wait_recv()
-            here = full.at[down(y, d), far(c)]
-            copy(2, 1, "y", d, here, here, c).wait_recv()
+        gathered(2, 0, full.at[others, near(c)], c)
+        gathered(2, 1, full.at[others, far(c)], c)
 
     whole = jnp.concatenate([full[j] for j in range(RING)], axis=1)
     parts = jnp.concatenate(three_parts(whole), axis=0)
@@ -250,9 +250,8 @@
         gram += dot_nt(full[j], full[j])
     state = eliminate(widen(gram), 0, rank // 2)
 
-    for d in ORDER[::-1]:
-        copy(3, 0, "z", d, fold_a.at[down(z, d)], fold_a.at[down(z, d)]).wait_recv()
-        copy(3, 1, "y", d, fold_b.at[down(y, d)], fold_b.at[down(y, d)]).wait_recv()
+    gathered(3, 0, fold_a.at[others])
+    gathered(3, 1, fold_b.at[others])
     total_a = fold_a[0]
     total_b = fold_b[0]
     for i in range(1, RING):
@@ -278,9 +277,8 @@
         picked += jnp.dot(parts, chosen, preferred_element_type=F32)
     picked = picked[:rank] + picked[rank : 2 * rank] + picked[2 * rank :]
 
-    for d in ORDER[::-1]:
-        copy(4, 0, "y", d, next_a.at[down(y, d)], next_a.at[down(y, d)]).wait_recv()
-        copy(4, 1, "z", d, next_b.at[down(z, d)], next_b.at[down(z, d)]).wait_recv()
+    gathered(4, 0, next_a.at[others])
+    gathered(4, 1, next_b.at[others])
     total_a = next_a[0]
     total_b = next_b[0]
     for i in range(1, RING):
@@ -313,8 +311,7 @@
         combined = g_ref[:, cols].astype(F32) + e_ref[:, cols].astype(F32)
         err_ref[:, cols] = (combined - approx).astype(BF16)
 
-    for d in ORDER[::-1]:
-        copy(5, 0, "s", d, norms.at[down(section, d)], norms.at[down(section, d)]).wait_recv()
+    gathered(5, 0, norms.at[others])
     squares = norms[0]
     for i in range(1, RING):
         squares += norms[i]
@@ -338,31 +335,46 @@
     mine = pl.ds(pl.multiple_of(y * width, 128), width)
     out_ref[0:rows, mine] = group_update(grad_a[...], pre_a).astype(BF16).T[0:rows]
 
-    hops = (
-        (2, 0, 0), (-2, 0, 0), (2, 0, 1), (-2, 0, 1), (1, 0, 0), (-1, 0, 0), (1, 0, 1), (-1, 0, 1),
-        (2, -2, 0), (1, -2, 0), (1, -2, 1), (-1, 2, 0), (-1, 2, 1), (-2, 2, 1),
-    )
+    if PIECES == 2:
+        hops = (
+            (2, 0, 0, 1), (-2, 0, 0, 1), (2, 0, 1, 1), (-2, 0, 1, 1),
+            (1, 0, 0, 1), (-1, 0, 0, 1), (1, 0, 1, 1), (-1, 0, 1, 1),
+            (2, -2, 0, 1), (1, -2, 0, 1), (1, -2, 1, 1), (-1, 2, 0, 1), (-1, 2, 1, 1), (-2, 2, 1, 1),
+        )
+        first, relay = 8, ((0, (8, 9)), (1, (11,)), (2, (10,)), (3, (13, 12)))
+    else:
+        hops = (
+            (2, 0, 0, 2), (-2, 0, 0, 2), (1, 0, 0, 2), (-1, 0, 0, 2),
+            (2, -2, 0, 1), (1, -2, 0, 2), (-2, 2, 1, 1), (-1, 2, 0, 2),
+        )
+        first, relay = 4, ((0, (4, 5)), (1, (6, 7)))
 
     def weight_copy(lane, sem, offset):
         axis, place = (("y", y), ("z", z))[lane]
-        target, _, part = hops[sem]
+        target, _, part, parts = hops[sem]
         block = up(place, offset % RING)
         if lane == 0:
             lanes = pl.ds(pl.multiple_of(block * width, 128), width)
-            view = out_ref.at[pl.ds(part * (rows // 2), rows // 2), lanes]
+            view = out_ref.at[pl.ds(part * (rows // 2), parts * (rows // 2)), lanes]
         else:
-            view = tail_b.at[block, pl.ds(3 * part, 3)]
-        return remote(7, lane, sem, axis, target % RING, view, view)
+            view = tail_b.at[block, pl.ds(3 * part, 3 * parts)]
+        came = weight_came.at[lane, min(sem, len(relay))]
+        return remote(weight_sent.at[lane], came, axis, target % RING, view, view)
+
+    def weight_view(lane, blocks):
+        return out_ref.at[pl.ds(0, rows), pl.ds(0, blocks * width)] if lane == 0 else tail_b.at[pl.ds(0, blocks)]
+
+    def weight_rest(lane):
+        view = weight_view(lane, RING - 3)
+        remote(weight_sent.at[lane], weight_came.at[lane, len(relay)], "z", 1, view, view).wait_recv()
 
     def weight_start(lane, sem):
-        c = weight_copy(lane, sem, hops[sem][1])
-        c.start()
-        started.append(c)
+        weight_copy(lane, sem, hops[sem][1]).start()
 
     def weight_landed(lane, sem):
         weight_copy(lane, sem, hops[sem][1] - hops[sem][0]).wait_recv()
 
-    for sem in range(8):
+    for sem in range(first):
         weight_start(0, sem)
     tail = group_update(grad_b[...], pre_b)
     lanes = lax.broadcasted_iota(jnp.int32, (owned, 128), 1)
@@ -371,7 +383,7 @@
         shift = rows - 32 * (i // 2)
         other = jnp.concatenate([other[:, 128 - shift :], other[:, : 128 - shift]], axis=1)
         tail_b[z, i] = jnp.where(lanes < rows, tail[i * owned : (i + 1) * owned], other).astype(BF16)
-    for sem in range(8):
+    for sem in range(first):
         weight_start(1, sem)
 
     own_a = grad_a[pl.ds(pl.multiple_of(z * owned, 8), owned)]
@@ -382,23 +394,26 @@
     new_first_ref[...] = new_first
     new_second_ref[...] = new_second
 
-    for sem, onward in ((0, (8, 9)), (1, (11,)), (2, (10,)), (3, (13, 12))):
+    for sem, onward in relay:
         for lane in (0, 1):
             weight_landed(lane, sem)
             for k in onward:
                 weight_start(lane, k)
-    for sem in range(4, 14):
-        weight_landed(1, sem)
+    weight_rest(1)
     for i in range(6):
         block = tail_b[:, i].reshape(width, 128).T
         out_ref[rows:, i * width : (i + 1) * width] = block[:rows]
         first_row = rows + 32 * (i // 2)
         first_col = (6 + i % 2) * width
         out_ref[first_row : first_row + 32, first_col : first_col + width] = block[rows:]
-    for sem in range(4, 14):
-        weight_landed(0, sem)
-    for c in started:
+    weight_rest(0)
+    for c in exchanges:
         c.wait_send()
+    for lane in range(2):
+        view = (pre_a, pre_b)[lane].at[others]
+        remote(state_sent.at[lane], state_came.at[lane, 0], "z", 1, view, view).wait_send()
+        view = weight_view(lane, RING - 1)
+        remote(weight_sent.at[lane], weight_came.at[lane, 0], "z", 1, view, view).wait_send()
 
 
 def finish_kernel(*refs):
@@ -456,8 +471,12 @@
             pltpu.VMEM((width, 128), F32),
             pltpu.VMEM((RING, 6, owned, 128), BF16),
             pltpu.SemaphoreType.DMA((8,)),
-            pltpu.SemaphoreType.DMA((8, 2, 2 * RING)),
-            pltpu.SemaphoreType.DMA((8, 2, 2 * RING)),
+            pltpu.SemaphoreType.DMA((6 * CHUNKS + 5,)),
+            pltpu.SemaphoreType.DMA((6 * CHUNKS + 5,)),
+            pltpu.SemaphoreType.DMA((2,)),
+            pltpu.SemaphoreType.DMA((2, 8)),
+            pltpu.SemaphoreType.DMA((2,)),
+            pltpu.SemaphoreType.DMA((2, 2 * PIECES + 1)),
         ],
         compiler_params=pltpu.CompilerParams(
             collective_id=0, has_side_effects=True, vmem_limit_bytes=40 << 20

time: 67.5 us -> 63.1 us (0.935)
  Pallas kernels: 66.7 us -> 62.3 us
    pallas_call x1, Pallas kernels: 65.1 us -> 60.8 us  [per_device(): pl.pallas_call(step_kernel, name='relay_step', out_shape=tuple((pltpu.VME...]
where the time goes in v4:
time: 63.1 us; the launch traced here: 63 us
  Pallas kernels  62.3 us (99%)
  between operations  0.64 us (1%)
    pallas_call x1, Pallas kernels, per_device(): pl.pallas_call(step_kernel, name='relay_step', out_shape=tuple((pltpu.VME...  60.8 us
    pallas_call x1, Pallas kernels, per_device(): pl.pallas_call(finish_kernel, name='finish', out_shape=shapes, in_specs=[...  1.52 us

profile of v4, /device:TPU:1, one launch (start us, length us, event | category | flops | bytes accessed | tf_op | source)
XLA Modules:
  0.0 63.0 jit_solution(10593379327812344092)
XLA Ops:
  0.6 60.8 %relay_step.1 = (bf16[192,3072]{1,0:T(8,128)(2,1)S(1)}, f32[32,192]{1,0:T(8,128)S(1)}, f32[48,192]{1,0:T(8,128)S(1)}, f32[48,192]{1,0:T(8,128)S(1)}, f32[48,192]...) custom-call(bf16[192,3072]{1,0:T(8,128)(2,1)} %bitcast.28, bf16[192,3072]{1,0:T(8,128)(2,1)} %bitcast.29, f32[32,192]{1,0:T(8,128)} %bitcast.33, ...), custom_call_target="tpu_custom_call" | custom-call | tf_op jit(solution)/shard_map/relay_step/pallas_call | solution.py:446
  61.5 1.5 %finish.1 = (bf16[192,3072]{1,0:T(8,128)(2,1)}, f32[32,192]{1,0:T(8,128)}, f32[48,192]{1,0:T(8,128)}, f32[48,192]{1,0:T(8,128)}, f32[48,192]{1,0:T(8,128)}, /*index=5*/bf16[192,3072]{1,0:T(8,128)(2,1)}) custom-call(bf16[192,3072]{1,0:T(8,128)(2,1)S(1)} %get-tuple-element.18.refs_0_, f32[32,192]{1,0:T(8,128)S(1)} %get-tuple-element.19.refs_1_, ...), custom_call_target="tpu_custom_call" | custom-call | tf_op jit(solution)/shard_map/finish/pallas_call | solution.py:485

commit v5 on v4

--- a/solution.py
+++ b/solution.py
@@ -72,8 +72,8 @@
 def step_kernel(
     g_hbm, e_hbm, q_hbm, master_hbm, first_hbm, second_hbm,
     err_ref, right_ref, new_master_ref, new_first_ref, new_second_ref, out_ref,
-    g_ref, e_ref, q_ref, states, local, red_a, red_b, sum_a, sum_b, full, fold_a, fold_b, next_a, next_b,
-    norms, pre_a, pre_b, grad_a, grad_b, tail_b, loads, sent, landed, state_sent, state_came, weight_sent, weight_came,
+    g_ref, e_ref, q_ref, states, local, red, sums, full, folds, nexts,
+    norms, pre, grad_a, grad_b, tail_b, tally, loads, sent, landed, state_came, weight_came,
 ):
     section = lax.axis_index("section")
     dp = lax.axis_index("dp")
@@ -99,87 +99,64 @@
             return (section, up(y, d) * RING + z)
         return (up(section, d), dp)
 
-    def remote(send_sem, recv_sem, axis, d, src, dst):
+    def remote(recv_sem, axis, d, src, dst):
         return pltpu.make_async_remote_copy(
-            src_ref=src, dst_ref=dst, send_sem=send_sem, recv_sem=recv_sem,
+            src_ref=src, dst_ref=dst, send_sem=sent.at[0], recv_sem=recv_sem,
             device_id=peer(axis, d), device_id_type=MESH,
         )
 
-    def slot(phase, lane, chunk):
-        return (2 * phase + lane) * CHUNKS + chunk if phase < 3 else 6 * CHUNKS + 2 * (phase - 3) + lane
-
-    def copy(phase, lane, axis, d, src, dst, chunk=0):
-        k = slot(phase, lane, chunk)
-        return remote(sent.at[k], landed.at[k], axis, d, src, dst)
-
-    exchanges = []
-
-    def send(*args):
-        copy(*args).start()
-
-    def gathered(phase, lane, view, chunk=0):
-        c = copy(phase, lane, "z", 1, view, view, chunk)
-        c.wait_recv()
-        exchanges.append(c)
+    def send(phase, axis, d, src, dst, chunk=0):
+        remote(landed.at[phase, chunk], axis, d, src, dst).start()
+
+    def gathered(phase, view, chunk=0):
+        remote(landed.at[phase, chunk], "z", 1, view, view).wait_recv()
+
+    middle = (RING // 2) * width
+    fetch = [(0, q_hbm, q_ref)]
+    for i in range(2):
+        cols = pl.ds(i * middle, middle)
+        fetch += [(1 + i, g_hbm.at[:, cols], g_ref.at[:, cols]), (1 + i, e_hbm.at[:, cols], e_ref.at[:, cols])]
+    fetch += [(3, x, states.at[i]) for i, x in enumerate((first_hbm, second_hbm, master_hbm))]
+    for i, x, v in fetch:
+        pltpu.make_async_copy(x, v, loads.at[i]).start()
+
+    def loaded(i, view):
+        pltpu.make_async_copy(view, view, loads.at[i]).wait()
 
     barrier = pltpu.get_barrier_semaphore()
     for axis in ("z", "y", "s"):
         for d in range(1, RING):
             pl.semaphore_signal(barrier, 1, device_id=peer(axis, d), device_id_type=MESH)
 
-    sources = [(q_hbm, q_ref)]
-    for i in range(2):
-        cols = pl.ds(i * (RING // 2) * width, (RING // 2) * width)
-        sources += [(g_hbm.at[:, cols], g_ref.at[:, cols]), (e_hbm.at[:, cols], e_ref.at[:, cols])]
-    sources += [(x, states.at[i]) for i, x in enumerate((first_hbm, second_hbm, master_hbm))]
-    fetch = [pltpu.make_async_copy(x, v, loads.at[i]) for i, (x, v) in enumerate(sources)]
-    for c in fetch:
-        c.start()
-    fetch[0].wait()
-
+    loaded(0, q_ref)
     parts = jnp.concatenate(three_parts(q_ref[...]), axis=0)
     for j in range(RING):
         if j % (RING // 2) == 0:
-            for c in fetch[1 + j // 2 : 3 + j // 2]:
-                c.wait()
+            loaded(1 + j // (RING // 2), g_ref)
         cols = pl.ds(j * width, width)
         term = jnp.dot(parts, g_ref[:, cols], preferred_element_type=F32)
         term += jnp.dot(parts, e_ref[:, cols], preferred_element_type=F32)
         local[j] = term[:rank] + term[rank : 2 * rank] + term[2 * rank :]
-    for c in fetch[5:]:
-        c.wait()
+    loaded(3, states)
     for i in range(3):
         value = states[i]
-        pre_a[z, i] = value[:, :128]
-        pre_b[y, i] = jnp.concatenate([value[:, rows:], value[:, : 128 - rows]], axis=1)
+        pre[0, z, i] = value[:, :128]
+        pre[1, y, i] = jnp.concatenate([value[:, rows:], value[:, : 128 - rows]], axis=1)
 
     pl.semaphore_wait(barrier, 3 * (RING - 1))
 
-    def state_copy(lane, step, way):
-        axis, place, buf = (("z", z, pre_a), ("y", y, pre_b))[lane]
-        block = down(place, step - 1) if way == 0 else up(place, step - 1)
-        view = buf.at[block]
-        if step == RING // 2:
-            part = owned // 2
-            view = buf.at[block, :, pl.ds(part * way, part)]
-        return remote(state_sent.at[lane], state_came.at[lane, way * 4 + step - 1], axis, 1 if way == 0 else RING - 1, view, view)
-
-    def state_landed(lane, step, way):
-        axis, place, buf = (("z", z, pre_a), ("y", y, pre_b))[lane]
-        block = down(place, step) if way == 0 else up(place, step)
-        view = buf.at[block]
-        if step == RING // 2:
-            part = owned // 2
-            view = buf.at[block, :, pl.ds(part * way, part)]
-        return remote(state_sent.at[lane], state_came.at[lane, way * 4 + step - 1], axis, 1 if way == 0 else RING - 1, view, view)
-
     def state_step(step):
-        for lane in range(2):
-            for way in range(2):
-                if step > 1:
-                    state_landed(lane, step - 1, way).wait_recv()
-                if step <= RING // 2:
-                    state_copy(lane, step, way).start()
+        if step > 1:
+            view = pre.at[0, pl.ds(0, 4 if step <= RING // 2 else 2)]
+            remote(state_came.at[step - 2], "z", 1, view, view).wait_recv()
+        if step > RING // 2:
+            return
+        for lane, (axis, place) in enumerate((("z", z), ("y", y))):
+            for way, block in enumerate((down(place, step - 1), up(place, step - 1))):
+                view = pre.at[lane, block]
+                if step == RING // 2:
+                    view = pre.at[lane, block, :, pl.ds(owned // 2 * way, owned // 2)]
+                remote(state_came.at[step - 1], axis, (1, RING - 1)[way], view, view).start()
 
     step = half // CHUNKS
     chunks = range(CHUNKS)
@@ -192,41 +169,38 @@
 
     for c in chunks:
         for d in ORDER:
-            send(0, 0, "z", d, local.at[up(z, d), near(c)], red_a.at[d - 1, near(c)], c)
-            send(0, 1, "y", d, local.at[up(y, d), far(c)], red_b.at[d - 1, near(c)], c)
+            send(0, "z", d, local.at[up(z, d), near(c)], red.at[0, d - 1, near(c)], c)
+            send(0, "y", d, local.at[up(y, d), far(c)], red.at[1, d - 1, near(c)], c)
     state_step(1)
     others = pl.ds(0, RING - 1)
     for c in chunks:
-        gathered(0, 0, red_a.at[:, near(c)], c)
-        gathered(0, 1, red_b.at[:, near(c)], c)
+        gathered(0, red.at[:, :, near(c)], c)
         total_a = local[z, near(c)]
         total_b = local[y, far(c)]
         for i in range(RING - 1):
-            total_a += red_a[i, near(c)]
-            total_b += red_b[i, near(c)]
-        sum_a[y, near(c)] = total_a
-        sum_b[z, near(c)] = total_b
+            total_a += red[0, i, near(c)]
+            total_b += red[1, i, near(c)]
+        sums[0, y, near(c)] = total_a
+        sums[1, z, near(c)] = total_b
         for d in ORDER:
-            send(1, 0, "y", d, sum_a.at[y, near(c)], sum_a.at[y, near(c)], c)
-            send(1, 1, "z", d, sum_b.at[z, near(c)], sum_b.at[z, near(c)], c)
+            send(1, "y", d, sums.at[0, y, near(c)], sums.at[0, y, near(c)], c)
+            send(1, "z", d, sums.at[1, z, near(c)], sums.at[1, z, near(c)], c)
     state_step(2)
     for c in chunks:
-        gathered(1, 0, sum_a.at[others, near(c)], c)
-        gathered(1, 1, sum_b.at[others, near(c)], c)
-        total_a = sum_a[0, near(c)]
-        total_b = sum_b[0, near(c)]
+        gathered(1, sums.at[:, others, near(c)], c)
+        total_a = sums[0, 0, near(c)]
+        total_b = sums[1, 0, near(c)]
         for i in range(1, RING):
-            total_a += sum_a[i, near(c)]
-            total_b += sum_b[i, near(c)]
+            total_a += sums[0, i, near(c)]
+            total_b += sums[1, i, near(c)]
         full[z, near(c)] = total_a
         full[y, far(c)] = total_b
         for d in ORDER:
-            send(2, 0, "z", d, full.at[z, near(c)], full.at[z, near(c)], c)
-            send(2, 1, "y", d, full.at[y, far(c)], full.at[y, far(c)], c)
+            send(2, "z", d, full.at[z, near(c)], full.at[z, near(c)], c)
+            send(2, "y", d, full.at[y, far(c)], full.at[y, far(c)], c)
     state_step(3)
     for c in chunks:
-        gathered(2, 0, full.at[others, near(c)], c)
-        gathered(2, 1, full.at[others, far(c)], c)
+        gathered(2, full.at[others, pl.ds(0, 2 * step)], c)
 
     whole = jnp.concatenate([full[j] for j in range(RING)], axis=1)
     parts = jnp.concatenate(three_parts(whole), axis=0)
@@ -236,13 +210,13 @@
     )
     right = right[:rank] + right[rank : 2 * rank] + right[2 * rank :]
     rest = jnp.concatenate([right[:half, 128:192], right[half:, 128:192]], axis=1)
-    fold_a[z, 0:16] = right[:half, :128]
-    fold_a[z, 16:24] = rest[:8]
-    fold_b[y, 0:16] = right[half:, :128]
-    fold_b[y, 16:24] = rest[8:]
+    folds[0, z, 0:16] = right[:half, :128]
+    folds[0, z, 16:24] = rest[:8]
+    folds[1, y, 0:16] = right[half:, :128]
+    folds[1, y, 16:24] = rest[8:]
     for d in ORDER:
-        send(3, 0, "z", d, fold_a.at[z], fold_a.at[z])
-        send(3, 1, "y", d, fold_b.at[y], fold_b.at[y])
+        send(3, "z", d, folds.at[0, z], folds.at[0, z])
+        send(3, "y", d, folds.at[1, y], folds.at[1, y])
     state_step(4)
 
     gram = jnp.zeros((rank, rank), F32)
@@ -250,18 +224,17 @@
         gram += dot_nt(full[j], full[j])
     state = eliminate(widen(gram), 0, rank // 2)
 
-    gathered(3, 0, fold_a.at[others])
-    gathered(3, 1, fold_b.at[others])
-    total_a = fold_a[0]
-    total_b = fold_b[0]
+    gathered(3, folds.at[:, others])
+    total_a = folds[0, 0]
+    total_b = folds[1, 0]
     for i in range(1, RING):
-        total_a += fold_a[i]
-        total_b += fold_b[i]
-    next_a[y] = total_a
-    next_b[z] = total_b
+        total_a += folds[0, i]
+        total_b += folds[1, i]
+    nexts[0, y] = total_a
+    nexts[1, z] = total_b
     for d in ORDER:
-        send(4, 0, "y", d, next_a.at[y], next_a.at[y])
-        send(4, 1, "z", d, next_b.at[z], next_b.at[z])
+        send(4, "y", d, nexts.at[0, y], nexts.at[0, y])
+        send(4, "z", d, nexts.at[1, z], nexts.at[1, z])
 
     wide, pivots = eliminate(state, rank // 2, rank)
     inverse = (wide * lax.rsqrt(pivots))[:, rank : 2 * rank]
@@ -277,13 +250,12 @@
         picked += jnp.dot(parts, chosen, preferred_element_type=F32)
     picked = picked[:rank] + picked[rank : 2 * rank] + picked[2 * rank :]
 
-    gathered(4, 0, next_a.at[others])
-    gathered(4, 1, next_b.at[others])
-    total_a = next_a[0]
-    total_b = next_b[0]
+    gathered(4, nexts.at[:, others])
+    total_a = nexts[0, 0]
+    total_b = nexts[1, 0]
     for i in range(1, RING):
-        total_a += next_a[i]
-        total_b += next_b[i]
+        total_a += nexts[0, i]
+        total_b += nexts[1, i]
     rest = jnp.concatenate([total_a[16:24], total_b[16:24]], axis=0)
     top = jnp.concatenate([total_a[0:16], total_b[0:16]], axis=0)
     rest = jnp.concatenate([rest[:, :64], rest[:, 64:]], axis=0)
@@ -292,7 +264,7 @@
     squares = jnp.sum(right * right, keepdims=True)
     norms[section] = jnp.broadcast_to(squares, (8, 128))
     for d in ORDER:
-        send(5, 0, "s", d, norms.at[section], norms.at[section])
+        send(5, "s", d, norms.at[section], norms.at[section])
     right_ref[...] = right
     state_step(5)
 
@@ -311,7 +283,7 @@
         combined = g_ref[:, cols].astype(F32) + e_ref[:, cols].astype(F32)
         err_ref[:, cols] = (combined - approx).astype(BF16)
 
-    gathered(5, 0, norms.at[others])
+    gathered(5, norms.at[others])
     squares = norms[0]
     for i in range(1, RING):
         squares += norms[i]
@@ -328,12 +300,12 @@
         )
         return master - learn_rate * adam_step, new_first, new_second
 
-    def group_update(grad, buf):
-        first, second, master = (buf[:, i].reshape(width, 128) for i in range(3))
+    def group_update(grad, lane):
+        first, second, master = (pre[lane, :, i].reshape(width, 128) for i in range(3))
         return update(grad, first, second, master)[0]
 
     mine = pl.ds(pl.multiple_of(y * width, 128), width)
-    out_ref[0:rows, mine] = group_update(grad_a[...], pre_a).astype(BF16).T[0:rows]
+    out_ref[0:rows, mine] = group_update(grad_a[...], 0).astype(BF16).T[0:rows]
 
     if PIECES == 2:
         hops = (
@@ -359,14 +331,14 @@
         else:
             view = tail_b.at[block, pl.ds(3 * part, 3 * parts)]
         came = weight_came.at[lane, min(sem, len(relay))]
-        return remote(weight_sent.at[lane], came, axis, target % RING, view, view)
+        return remote(came, axis, target % RING, view, view)
 
     def weight_view(lane, blocks):
         return out_ref.at[pl.ds(0, rows), pl.ds(0, blocks * width)] if lane == 0 else tail_b.at[pl.ds(0, blocks)]
 
     def weight_rest(lane):
         view = weight_view(lane, RING - 3)
-        remote(weight_sent.at[lane], weight_came.at[lane, len(relay)], "z", 1, view, view).wait_recv()
+        remote(weight_came.at[lane, len(relay)], "z", 1, view, view).wait_recv()
 
     def weight_start(lane, sem):
         weight_copy(lane, sem, hops[sem][1]).start()
@@ -376,7 +348,7 @@
 
     for sem in range(first):
         weight_start(0, sem)
-    tail = group_update(grad_b[...], pre_b)
+    tail = group_update(grad_b[...], 1)
     lanes = lax.broadcasted_iota(jnp.int32, (owned, 128), 1)
     for i in range(6):
         other = tail[(6 + i % 2) * owned : (7 + i % 2) * owned]
@@ -394,11 +366,12 @@
     new_first_ref[...] = new_first
     new_second_ref[...] = new_second
 
-    for sem, onward in relay:
+    for pair in (relay[:2], relay[2:]):
         for lane in (0, 1):
-            weight_landed(lane, sem)
-            for k in onward:
-                weight_start(lane, k)
+            for sem, onward in pair:
+                weight_landed(lane, sem)
+                for k in onward:
+                    weight_start(lane, k)
     weight_rest(1)
     for i in range(6):
         block = tail_b[:, i].reshape(width, 128).T
@@ -407,13 +380,7 @@
         first_col = (6 + i % 2) * width
         out_ref[first_row : first_row + 32, first_col : first_col + width] = block[rows:]
     weight_rest(0)
-    for c in exchanges:
-        c.wait_send()
-    for lane in range(2):
-        view = (pre_a, pre_b)[lane].at[others]
-        remote(state_sent.at[lane], state_came.at[lane, 0], "z", 1, view, view).wait_send()
-        view = weight_view(lane, RING - 1)
-        remote(weight_sent.at[lane], weight_came.at[lane, 0], "z", 1, view, view).wait_send()
+    remote(weight_came.at[0, 0], "z", 1, tally, tally).wait_send()
 
 
 def finish_kernel(*refs):
@@ -431,6 +398,9 @@
     owned = master.shape[2]
     half = rank // 2
     width = cols // RING
+    blocks = 2 * (RING - 1)
+    exchanged = 3 * half * width + 2 * 24 * 128 + 4 * 128 + 3 * owned * 128 + rows // 2 * width // 2
+    tally_rows = blocks * exchanged // 128
     vmem = pl.BlockSpec(memory_space=pltpu.VMEM)
     hbm = pl.BlockSpec(memory_space=pltpu.HBM)
     shapes = (
@@ -455,27 +425,21 @@
             pltpu.VMEM((rank, rows), F32),
             pltpu.VMEM((3, owned, rows), F32),
             pltpu.VMEM((RING, rank, width), F32),
-            pltpu.VMEM((RING - 1, half, width), F32),
-            pltpu.VMEM((RING - 1, half, width), F32),
-            pltpu.VMEM((RING, half, width), F32),
-            pltpu.VMEM((RING, half, width), F32),
+            pltpu.VMEM((2, RING - 1, half, width), F32),
+            pltpu.VMEM((2, RING, half, width), F32),
             pltpu.VMEM((RING, rank, width), F32),
-            pltpu.VMEM((RING, 24, 128), F32),
-            pltpu.VMEM((RING, 24, 128), F32),
-            pltpu.VMEM((RING, 24, 128), F32),
-            pltpu.VMEM((RING, 24, 128), F32),
+            pltpu.VMEM((2, RING, 24, 128), F32),
+            pltpu.VMEM((2, RING, 24, 128), F32),
             pltpu.VMEM((RING, 8, 128), F32),
-            pltpu.VMEM((RING, 3, owned, 128), F32),
-            pltpu.VMEM((RING, 3, owned, 128), F32),
+            pltpu.VMEM((2, RING, 3, owned, 128), F32),
             pltpu.VMEM((width, 128), F32),
             pltpu.VMEM((width, 128), F32),
             pltpu.VMEM((RING, 6, owned, 128), BF16),
-            pltpu.SemaphoreType.DMA((8,)),
-            pltpu.SemaphoreType.DMA((6 * CHUNKS + 5,)),
-            pltpu.SemaphoreType.DMA((6 * CHUNKS + 5,)),
-            pltpu.SemaphoreType.DMA((2,)),
-            pltpu.SemaphoreType.DMA((2, 8)),
-            pltpu.SemaphoreType.DMA((2,)),
+            pltpu.VMEM((tally_rows, 128), F32),
+            pltpu.SemaphoreType.DMA((4,)),
+            pltpu.SemaphoreType.DMA((1,)),
+            pltpu.SemaphoreType.DMA((6, CHUNKS)),
+            pltpu.SemaphoreType.DMA((4,)),
             pltpu.SemaphoreType.DMA((2, 2 * PIECES + 1)),
         ],
         compiler_params=pltpu.CompilerParams(

time: 63.1 us -> 62.2 us (0.986)
  Pallas kernels: 62.3 us -> 61.4 us
    pallas_call x1, Pallas kernels: 60.8 us -> 59.9 us  [per_device(): pl.pallas_call(step_kernel, name='relay_step', out_shape=tuple((pltpu.VME...]
where the time goes in v5:
time: 62.2 us; the launch traced here: 62 us
  Pallas kernels  61.4 us (99%)
  between operations  0.64 us (1%)
    pallas_call x1, Pallas kernels, per_device(): pl.pallas_call(step_kernel, name='relay_step', out_shape=tuple((pltpu.VME...  59.9 us
    pallas_call x1, Pallas kernels, per_device(): pl.pallas_call(finish_kernel, name='finish', out_shape=shapes, in_specs=[...  1.52 us

profile of v5, /device:TPU:1, one launch (start us, length us, event | category | flops | bytes accessed | tf_op | source)
XLA Modules:
  0.0 62.0 jit_solution(11242855572489705785)
XLA Ops:
  0.6 59.9 %relay_step.1 = (bf16[192,3072]{1,0:T(8,128)(2,1)S(1)}, f32[32,192]{1,0:T(8,128)S(1)}, f32[48,192]{1,0:T(8,128)S(1)}, f32[48,192]{1,0:T(8,128)S(1)}, f32[48,192]...) custom-call(bf16[192,3072]{1,0:T(8,128)(2,1)} %bitcast.28, bf16[192,3072]{1,0:T(8,128)(2,1)} %bitcast.29, f32[32,192]{1,0:T(8,128)} %bitcast.33, ...), custom_call_target="tpu_custom_call" | custom-call | tf_op jit(solution)/shard_map/relay_step/pallas_call | solution.py:416
  60.5 1.5 %finish.1 = (bf16[192,3072]{1,0:T(8,128)(2,1)}, f32[32,192]{1,0:T(8,128)}, f32[48,192]{1,0:T(8,128)}, f32[48,192]{1,0:T(8,128)}, f32[48,192]{1,0:T(8,128)}, /*index=5*/bf16[192,3072]{1,0:T(8,128)(2,1)}) custom-call(bf16[192,3072]{1,0:T(8,128)(2,1)S(1)} %get-tuple-element.18.refs_0_, f32[32,192]{1,0:T(8,128)S(1)} %get-tuple-element.19.refs_1_, ...), custom_call_target="tpu_custom_call" | custom-call | tf_op jit(solution)/shard_map/finish/pallas_call | solution.py:449

commit v6 on v5

--- a/solution.py
+++ b/solution.py
@@ -17,7 +17,9 @@
 clip_limit = 16.0
 
 RING = 8
-CHUNKS = 2
+ROW_CHUNKS = 2
+LANE_CHUNKS = 1
+CHUNKS = ROW_CHUNKS * LANE_CHUNKS
 PIECES = 2
 ORDER = (4, 3, 5, 2, 6, 1, 7)
 MESH = pl.DeviceIdType.MESH
@@ -137,12 +139,6 @@
         term = jnp.dot(parts, g_ref[:, cols], preferred_element_type=F32)
         term += jnp.dot(parts, e_ref[:, cols], preferred_element_type=F32)
         local[j] = term[:rank] + term[rank : 2 * rank] + term[2 * rank :]
-    loaded(3, states)
-    for i in range(3):
-        value = states[i]
-        pre[0, z, i] = value[:, :128]
-        pre[1, y, i] = jnp.concatenate([value[:, rows:], value[:, : 128 - rows]], axis=1)
-
     pl.semaphore_wait(barrier, 3 * (RING - 1))
 
     def state_step(step):
@@ -158,49 +154,55 @@
                     view = pre.at[lane, block, :, pl.ds(owned // 2 * way, owned // 2)]
                 remote(state_came.at[step - 1], axis, (1, RING - 1)[way], view, view).start()
 
-    step = half // CHUNKS
+    step = half // ROW_CHUNKS
+    span = width // LANE_CHUNKS
     chunks = range(CHUNKS)
 
     def near(c):
-        return pl.ds(c * step, step)
+        return pl.ds(c // LANE_CHUNKS * step, step), pl.ds(c % LANE_CHUNKS * span, span)
 
     def far(c):
-        return pl.ds(half + c * step, step)
+        return pl.ds(half + c // LANE_CHUNKS * step, step), pl.ds(c % LANE_CHUNKS * span, span)
 
     for c in chunks:
         for d in ORDER:
-            send(0, "z", d, local.at[up(z, d), near(c)], red.at[0, d - 1, near(c)], c)
-            send(0, "y", d, local.at[up(y, d), far(c)], red.at[1, d - 1, near(c)], c)
+            send(0, "z", d, local.at[up(z, d), *near(c)], red.at[0, d - 1, *near(c)], c)
+            send(0, "y", d, local.at[up(y, d), *far(c)], red.at[1, d - 1, *near(c)], c)
+    loaded(3, states)
+    for i in range(3):
+        value = states[i]
+        pre[0, z, i] = value[:, :128]
+        pre[1, y, i] = jnp.concatenate([value[:, rows:], value[:, : 128 - rows]], axis=1)
     state_step(1)
     others = pl.ds(0, RING - 1)
     for c in chunks:
-        gathered(0, red.at[:, :, near(c)], c)
-        total_a = local[z, near(c)]
-        total_b = local[y, far(c)]
+        gathered(0, red.at[:, :, *near(c)], c)
+        total_a = local[z, *near(c)]
+        total_b = local[y, *far(c)]
         for i in range(RING - 1):
-            total_a += red[0, i, near(c)]
-            total_b += red[1, i, near(c)]
-        sums[0, y, near(c)] = total_a
-        sums[1, z, near(c)] = total_b
+            total_a += red[0, i, *near(c)]
+            total_b += red[1, i, *near(c)]
+        sums[0, y, *near(c)] = total_a
+        sums[1, z, *near(c)] = total_b
         for d in ORDER:
-            send(1, "y", d, sums.at[0, y, near(c)], sums.at[0, y, near(c)], c)
-            send(1, "z", d, sums.at[1, z, near(c)], sums.at[1, z, near(c)], c)
+            send(1, "y", d, sums.at[0, y, *near(c)], sums.at[0, y, *near(c)], c)
+            send(1, "z", d, sums.at[1, z, *near(c)], sums.at[1, z, *near(c)], c)
     state_step(2)
     for c in chunks:
-        gathered(1, sums.at[:, others, near(c)], c)
-        total_a = sums[0, 0, near(c)]
-        total_b = sums[1, 0, near(c)]
+        gathered(1, sums.at[:, others, *near(c)], c)
+        total_a = sums[0, 0, *near(c)]
+        total_b = sums[1, 0, *near(c)]
         for i in range(1, RING):
-            total_a += sums[0, i, near(c)]
-            total_b += sums[1, i, near(c)]
-        full[z, near(c)] = total_a
-        full[y, far(c)] = total_b
+            total_a += sums[0, i, *near(c)]
+            total_b += sums[1, i, *near(c)]
+        full[z, *near(c)] = total_a
+        full[y, *far(c)] = total_b
         for d in ORDER:
-            send(2, "z", d, full.at[z, near(c)], full.at[z, near(c)], c)
-            send(2, "y", d, full.at[y, far(c)], full.at[y, far(c)], c)
+            send(2, "z", d, full.at[z, *near(c)], full.at[z, *near(c)], c)
+            send(2, "y", d, full.at[y, *far(c)], full.at[y, *far(c)], c)
     state_step(3)
     for c in chunks:
-        gathered(2, full.at[others, pl.ds(0, 2 * step)], c)
+        gathered(2, full.at[others, pl.ds(0, 2 * step), pl.ds(0, span)], c)
 
     whole = jnp.concatenate([full[j] for j in range(RING)], axis=1)
     parts = jnp.concatenate(three_parts(whole), axis=0)
@@ -293,12 +295,9 @@
         scaled = clip * grad
         new_first = beta_one * first + (1.0 - beta_one) * scaled
         new_second = beta_two * second + (1.0 - beta_two) * scaled * scaled
-        adam_step = (
-            new_first
-            / (1.0 - beta_one**STEP)
-            / (jnp.sqrt(new_second / (1.0 - beta_two**STEP)) + adam_epsilon)
-        )
-        return master - learn_rate * adam_step, new_first, new_second
+        rate = learn_rate / (1.0 - beta_one**STEP)
+        spread = jnp.sqrt(new_second * (1.0 / (1.0 - beta_two**STEP))) + adam_epsilon
+        return master - rate * new_first / spread, new_first, new_second
 
     def group_update(grad, lane):
         first, second, master = (pre[lane, :, i].reshape(width, 128) for i in range(3))

time: 62.2 us -> 61.9 us (level)
  no operation moved by 1% of the time
where the time goes in v6:
time: 61.9 us; the launch traced here: 61.7 us
  Pallas kernels  61.1 us (99%)
  between operations  0.64 us (1%)
    pallas_call x1, Pallas kernels, per_device(): pl.pallas_call(step_kernel, name='relay_step', out_shape=tuple((pltpu.VME...  59.5 us
    pallas_call x1, Pallas kernels, per_device(): pl.pallas_call(finish_kernel, name='finish', out_shape=shapes, in_specs=[...  1.52 us

profile of v6, /device:TPU:1, one launch (start us, length us, event | category | flops | bytes accessed | tf_op | source)
XLA Modules:
  0.0 61.7 jit_solution(10855857399358163168)
XLA Ops:
  0.6 59.5 %relay_step.1 = (bf16[192,3072]{1,0:T(8,128)(2,1)S(1)}, f32[32,192]{1,0:T(8,128)S(1)}, f32[48,192]{1,0:T(8,128)S(1)}, f32[48,192]{1,0:T(8,128)S(1)}, f32[48,192]...) custom-call(bf16[192,3072]{1,0:T(8,128)(2,1)} %bitcast.28, bf16[192,3072]{1,0:T(8,128)(2,1)} %bitcast.29, f32[32,192]{1,0:T(8,128)} %bitcast.33, ...), custom_call_target="tpu_custom_call" | custom-call | tf_op jit(solution)/shard_map/relay_step/pallas_call | solution.py:415
  60.2 1.5 %finish.1 = (bf16[192,3072]{1,0:T(8,128)(2,1)}, f32[32,192]{1,0:T(8,128)}, f32[48,192]{1,0:T(8,128)}, f32[48,192]{1,0:T(8,128)}, f32[48,192]{1,0:T(8,128)}, /*index=5*/bf16[192,3072]{1,0:T(8,128)(2,1)}) custom-call(bf16[192,3072]{1,0:T(8,128)(2,1)S(1)} %get-tuple-element.18.refs_0_, f32[32,192]{1,0:T(8,128)S(1)} %get-tuple-element.19.refs_1_, ...), custom_call_target="tpu_custom_call" | custom-call | tf_op jit(solution)/shard_map/finish/pallas_call | solution.py:448

commit v7 on v6

--- a/solution.py
+++ b/solution.py
@@ -75,7 +75,7 @@
     g_hbm, e_hbm, q_hbm, master_hbm, first_hbm, second_hbm,
     err_ref, right_ref, new_master_ref, new_first_ref, new_second_ref, out_ref,
     g_ref, e_ref, q_ref, states, local, red, sums, full, folds, nexts,
-    norms, pre, grad_a, grad_b, tail_b, tally, loads, sent, landed, state_came, weight_came,
+    norms, pre, grad_a, grad_b, terms, tail_b, tally, loads, sent, landed, state_came, weight_came,
 ):
     section = lax.axis_index("section")
     dp = lax.axis_index("dp")
@@ -273,6 +273,12 @@
     coef = dot_tn(inverse, right)
     grad_a[...] = dot_tn(full[y], coef[:, :128])
     grad_b[...] = dot_tn(picked, jnp.concatenate([coef[:, rows:], coef[:, : 128 - rows]], axis=1))
+    rate = learn_rate / (1.0 - beta_one**STEP)
+    gain = 1.0 / (1.0 - beta_two**STEP)
+    for lane, grad in enumerate((grad_a, grad_b)):
+        terms[lane, 0] = (rate * beta_one) * pre[lane, :, 0].reshape(width, 128)
+        terms[lane, 1] = (gain * beta_two) * pre[lane, :, 1].reshape(width, 128)
+        terms[lane, 2] = grad[...] * grad[...]
     high, low, _ = three_parts(coef)
     left = jnp.concatenate([high, high, low], axis=0)
     for j in range(RING):
@@ -295,13 +301,13 @@
         scaled = clip * grad
         new_first = beta_one * first + (1.0 - beta_one) * scaled
         new_second = beta_two * second + (1.0 - beta_two) * scaled * scaled
-        rate = learn_rate / (1.0 - beta_one**STEP)
-        spread = jnp.sqrt(new_second * (1.0 / (1.0 - beta_two**STEP))) + adam_epsilon
+        spread = jnp.sqrt(new_second * gain) + adam_epsilon
         return master - rate * new_first / spread, new_first, new_second
 
     def group_update(grad, lane):
-        first, second, master = (pre[lane, :, i].reshape(width, 128) for i in range(3))
-        return update(grad, first, second, master)[0]
+        move = terms[lane, 0] + (rate * (1.0 - beta_one) * clip) * grad
+        spread = jnp.sqrt(terms[lane, 1] + (gain * (1.0 - beta_two) * clip * clip) * terms[lane, 2]) + adam_epsilon
+        return pre[lane, :, 2].reshape(width, 128) - move / spread
 
     mine = pl.ds(pl.multiple_of(y * width, 128), width)
     out_ref[0:rows, mine] = group_update(grad_a[...], 0).astype(BF16).T[0:rows]
@@ -433,6 +439,7 @@
             pltpu.VMEM((2, RING, 3, owned, 128), F32),
             pltpu.VMEM((width, 128), F32),
             pltpu.VMEM((width, 128), F32),
+            pltpu.VMEM((2, 3, width, 128), F32),
             pltpu.VMEM((RING, 6, owned, 128), BF16),
             pltpu.VMEM((tally_rows, 128), F32),
             pltpu.SemaphoreType.DMA((4,)),

time: 61.9 us -> 61.8 us (level)
  no operation moved by 1% of the time
where the time goes in v7:
time: 61.8 us; the launch traced here: 61.7 us
  Pallas kernels  61 us (99%)
  between operations  0.64 us (1%)
    pallas_call x1, Pallas kernels, per_device(): pl.pallas_call(step_kernel, name='relay_step', out_shape=tuple((pltpu.VME...  59.5 us
    pallas_call x1, Pallas kernels, per_device(): pl.pallas_call(finish_kernel, name='finish', out_shape=shapes, in_specs=[...  1.52 us

profile of v7, /device:TPU:1, one launch (start us, length us, event | category | flops | bytes accessed | tf_op | source)
XLA Modules:
  0.0 61.7 jit_solution(3312913932964455578)
XLA Ops:
  0.6 59.5 %relay_step.1 = (bf16[192,3072]{1,0:T(8,128)(2,1)S(1)}, f32[32,192]{1,0:T(8,128)S(1)}, f32[48,192]{1,0:T(8,128)S(1)}, f32[48,192]{1,0:T(8,128)S(1)}, f32[48,192]...) custom-call(bf16[192,3072]{1,0:T(8,128)(2,1)} %bitcast.28, bf16[192,3072]{1,0:T(8,128)(2,1)} %bitcast.29, f32[32,192]{1,0:T(8,128)} %bitcast.33, ...), custom_call_target="tpu_custom_call" | custom-call | tf_op jit(solution)/shard_map/relay_step/pallas_call | solution.py:421
  60.2 1.5 %finish.1 = (bf16[192,3072]{1,0:T(8,128)(2,1)}, f32[32,192]{1,0:T(8,128)}, f32[48,192]{1,0:T(8,128)}, f32[48,192]{1,0:T(8,128)}, f32[48,192]{1,0:T(8,128)}, /*index=5*/bf16[192,3072]{1,0:T(8,128)(2,1)}) custom-call(bf16[192,3072]{1,0:T(8,128)(2,1)S(1)} %get-tuple-element.18.refs_0_, f32[32,192]{1,0:T(8,128)S(1)} %get-tuple-element.19.refs_1_, ...), custom_call_target="tpu_custom_call" | custom-call | tf_op jit(solution)/shard_map/finish/pallas_call | solution.py:455
